TPU v7x, 256 devices: a whole 4x4x8 slice. The times are simulated.
256 devices in a mesh: row: 4 (over y), col: 8 (over z), lag: 8 (over x, core).
Axes of the slice: x: 4, y: 4, z: 8, core: 2. Of those that a mesh axis runs over, the one named last changes fastest.
Arguments:
- history: float32 [32, 256, 128], P(None, ('row', 'col', 'lag')), may hold values from -6 to 6
- step_index: int32 [1], replicated, may hold values from 0 to 31
- pair_rows: int32 [4, 8, 32], P('row', 'col'), may hold values from 0 to 63, as said below
- pair_cols: int32 [4, 8, 32], P('row', 'col'), may hold values from 0 to 31, as said below
- lag_pattern: int32 [4, 8, 32, 32], P('row', 'col', None, 'lag'), may hold values 0 or 1
- blocks: float32 [4, 8, 32, 32, 128, 128], P('row', 'col', None, 'lag'), may hold values from -0.1875 to 0.1875
- incident: float32 [256, 128], P(('row', 'col', 'lag')), may hold values from -6 to 6
- self_inverse: float32 [256, 128, 128], P(('row', 'col', 'lag')), may hold values from -0.5 to 0.5
Outputs:
- new_field: float32 [256, 128], P(('row', 'col', 'lag'))
Inputs may be any that keep to these rules, and one draw needn't show every extreme that they name: `pair_cols`: see pair_rows.
All inputs are finite; a program needn't handle non-finite values. No bound on the sum of `lag_pattern` on one device may be relied on, other than what follows from the above.
Results may differ from a plain program's by a relative error of at most 0.0003.
Values sent between devices are 32-bit elements; how exact they have to be, the bound alone decides.
No kernel may reach another device: no remote copies, remote signals or barrier semaphores. Data moves between devices by JAX's collectives and lax.ppermute only.
A program may use at most 64 MiB of HBM per device.

v0:
```python
import jax
import jax.numpy as jnp
from jax import lax
from jax.sharding import PartitionSpec as P


def per_device(
    history, step_index, pair_rows, pair_cols, lag_pattern, blocks, incident, self_inverse
):
    row_count = lax.axis_size("row")
    col_count = lax.axis_size("col")
    lag_count = lax.axis_size("lag")
    lags_all = history.shape[0]
    sub_blocks = history.shape[1]
    lag_local = blocks.shape[3]
    group_size = sub_blocks * lag_count
    row_band = group_size * col_count
    col_band = group_size * row_count
    row_index = lax.axis_index("row")
    col_index = lax.axis_index("col")
    lag_index = lax.axis_index("lag")
    own_lags = lag_index * lag_local + jnp.arange(lag_local, dtype=jnp.int32)
    slot_ids = jnp.mod(step_index[0] - 1 - own_lags, lags_all)
    row_source = jnp.take(
        lax.all_gather(history, ("col", "lag"), axis=1, tiled=True), slot_ids, axis=0
    )
    col_source = jnp.take(
        lax.all_gather(history, ("row", "lag"), axis=1, tiled=True), slot_ids, axis=0
    )
    rows_local = pair_rows[0, 0]
    cols_local = pair_cols[0, 0]
    matrices = blocks[0, 0]
    lag_mask = lag_pattern[0, 0].astype(jnp.float32)
    row_vectors = jnp.take(row_source, rows_local, axis=1)
    col_vectors = jnp.take(col_source, cols_local, axis=1)
    forward = jnp.einsum(
        "plab,lpb,pl->pa", matrices, col_vectors, lag_mask, precision=lax.Precision.HIGHEST
    )
    row_global = row_index * row_band + rows_local
    col_global = (
        cols_local // group_size * row_band + col_index * group_size + cols_local % group_size
    )
    off_diag = jnp.where(row_global != col_global, 1.0, 0.0).astype(jnp.float32)
    mirror = jnp.einsum(
        "plab,lpa,pl->pb", matrices, row_vectors, lag_mask, precision=lax.Precision.HIGHEST
    )
    mirror = mirror * off_diag[:, None]
    row_hits = (rows_local[:, None] == jnp.arange(row_band, dtype=jnp.int32)[None, :]).astype(
        jnp.float32
    )
    col_hits = (cols_local[:, None] == jnp.arange(col_band, dtype=jnp.int32)[None, :]).astype(
        jnp.float32
    )
    row_fields = jnp.dot(row_hits.T, forward, precision=lax.Precision.HIGHEST)
    col_fields = jnp.dot(col_hits.T, mirror, precision=lax.Precision.HIGHEST)
    row_part = lax.psum_scatter(row_fields, "col", scatter_dimension=0, tiled=True)
    col_part = lax.psum_scatter(col_fields, "row", scatter_dimension=0, tiled=True)
    convolved = lax.psum_scatter(row_part + col_part, "lag", scatter_dimension=0, tiled=True)
    return jnp.einsum(
        "bxy,by->bx", self_inverse, incident - convolved, precision=lax.Precision.HIGHEST
    )


def solution(mesh):
    in_specs = (
        P(None, ("row", "col", "lag"), None),
        P(),
        P("row", "col", None),
        P("row", "col", None),
        P("row", "col", None, "lag"),
        P("row", "col", None, "lag", None, None),
        P(("row", "col", "lag"), None),
        P(("row", "col", "lag"), None, None),
    )
    out_specs = P(("row", "col", "lag"), None)
    return jax.shard_map(
        per_device, mesh=mesh, in_specs=in_specs, out_specs=out_specs, check_vma=False
    )
```

profile of v0, /device:TPU:1, one launch (start us, length us, event | category | flops | bytes accessed | tf_op | source)
XLA Modules:
  0.0 174.9 jit_solution(8708508319175010513)
XLA Ops:
  6.5 0.0 copy-start
  6.5 0.0 all-gather.2.cloned.1.call-start
  6.5 0.7 all-gather.2.cloned.1.call-update
  7.9 1.3 dynamic-slice.4
  9.2 1.3 dynamic-slice.2
  10.5 1.3 dynamic-slice
  13.1 0.7 convert_bitcast_fusion
  13.8 0.1 copy.16
  13.9 26.4 %all_gather.6 = f32[32,32,128]{2,0,1:T(8,128)S(1)} all-gather(f32[32,1,128]{2,0,1:T(8,128)} %bitcast.55), channel_id=1, replica_groups=mesh['row'=4,'col'=8,'lag'=8] {'row','lag'}, dimensions={1}, use_global_device_ids=true | all-gather | bytes 540672 | tf_op jit(solution)/shard_map/all_gather | solution.py:28
  40.3 0.3 copy.14
  40.6 0.6 gather_fusion
  41.2 0.1 broadcast_select_fusion.1
  41.3 0.7 fusion.19
  42.0 0.6 gather_fusion.1
  42.6 0.7 fusion.20
  43.3 0.7 compare_select_fusion.9
  44.0 0.7 compare_and_fusion
  44.7 46.0 %all-gather.2.cloned.1.call-done = f32[32,64,128]{2,0,1:T(8,128)} async-done(((f32[32,1,128]{2,0,1:T(8,128)}), f32[32,64,128]{2,0,1:T(8,128)}) %all-gather.2.cloned.1.call-update) | async-done | bytes 1048592 | tf_op jit(solution)/shard_map/all_gather | solution.py:25
  90.7 1.8 %copy.18 = f32[32,64,128]{2,1,0:T(8,128)S(1)} copy(f32[32,64,128]{2,0,1:T(8,128)} %all-gather.2.cloned.1.call-done) | data formatting | bytes 2097152 | tf_op jit(solution)/shard_map/all_gather | solution.py:25
  92.5 0.6 gather_fusion.2
  93.1 0.1 broadcast_select_fusion
  93.2 0.1 copy.19
  93.3 0.6 gather_fusion.3
  93.9 0.0 copy-start.1
  93.9 0.2 select_multiply_fusion.1
  94.1 0.0 copy-start.2
  94.1 0.0 copy-start.3
  94.1 0.0 copy-start.4
  94.1 10.1 %fusion.2 = f32[32,1,128,1]{2,1,3,0:T(1,128)S(1)} fusion(f32[32,4,128,1]{2,3,1,0:T(1,128)S(1)} %bitcast.53, f32[1,1,32,4,128,128]{5,4,3,2,1,0:T(8,128)} %param.13), kind=kOutput, calls=%fused_computation.6 | convolution fusion | flops 25165824 | bytes 8470528 | tf_op jit(solution)/shard_map/plab,lpb,pl->pa/dot_general | solution.py:36
  104.3 0.0 copy-done.1
  104.3 4.2 %fusion = f32[32,1,128,1]{2,1,3,0:T(1,128)S(1)} fusion(f32[32,4,128,1]{2,3,1,0:T(1,128)S(1)} %bitcast.52, f32[1,1,32,4,128,128]{5,4,3,2,1,0:T(8,128)S(1)} %copy-done.1), kind=kOutput, calls=%fused_computation.4 | convolution fusion | flops 25165824 | bytes 8470528 | tf_op jit(solution)/shard_map/plab,lpa,pl->pb/dot_general | solution.py:44
  108.4 0.0 copy-done.2
  108.4 0.3 fusion.6
  108.7 13.1 %all-reduce.1 = f32[32,128]{1,0:T(8,128)S(1)} all-reduce(f32[32,128]{1,0:T(8,128)S(1)} %fusion.6), channel_id=3, replica_groups=mesh['row'=4,'col'=8,'lag'=8] {'row'}, use_global_device_ids=true, to_apply=%region_1.2.clone | all-reduce | flops 4096 | bytes 32768
  121.8 0.0 copy-done.3
  121.8 0.3 fusion.8
  122.1 21.6 %all-reduce = f32[64,128]{1,0:T(8,128)S(1)} all-reduce(f32[64,128]{1,0:T(8,128)S(1)} %fusion.8), channel_id=2, replica_groups=mesh['row'=4,'col'=8,'lag'=8] {'col'}, use_global_device_ids=true, to_apply=%region_0.1.clone | all-reduce | flops 8192 | bytes 65536
  143.7 22.9 %all-reduce.2 = f32[8,128]{1,0:T(8,128)S(1)} all-reduce(f32[8,128]{1,0:T(8,128)S(1)} %dynamic-slice_add_fusion), channel_id=4, replica_groups=mesh['row'=4,'col'=8,'lag'=8] {'lag'}, use_global_device_ids=true, to_apply=%region_2.3.clone | all-reduce | flops 1024 | bytes 8192
  166.7 0.0 copy-done
  166.7 0.0 copy-done.4
  166.7 1.4 fusion.4
  (7 shorter events, 0.1 us)
Async XLA Ops:
  6.5 160.1 %copy-start = (f32[1,128,128]{2,1,0:T(8,128)S(1)}, f32[1,128,128]{2,1,0:T(8,128)}, u32[]{:S(2)}) copy-start(f32[1,128,128]{2,1,0:T(8,128)} %param.15) | copy-start | bytes 196612
  6.5 84.2 %all-gather.2.cloned.1.call-start = ((), (), s32[]{:S(2)}) async-start(), calls=%async_computation | async-start | bytes 1064960 | tf_op jit(solution)/shard_map/all_gather | solution.py:25
  93.9 10.4 %copy-start.1 = (f32[1,1,32,4,128,128]{5,4,3,2,1,0:T(8,128)S(1)}, f32[1,1,32,4,128,128]{5,4,3,2,1,0:T(8,128)}, u32[]{:S(2)}) copy-start(f32[1,1,32,4,128,128]{5,4,3,2,1,0:T(8,128)} %param.13) | copy-start | bytes 25165828
  94.1 14.3 %copy-start.2 = (s32[1,1,32]{2,1,0:T(1,128)S(1)}, s32[1,1,32]{2,1,0:T(1,128)}, u32[]{:S(2)}) copy-start(s32[1,1,32]{2,1,0:T(1,128)} %param.11) | copy-start | bytes 388
  94.1 27.7 %copy-start.3 = (s32[1,1,32]{2,1,0:T(1,128)S(1)}, s32[1,1,32]{2,1,0:T(1,128)}, u32[]{:S(2)}) copy-start(s32[1,1,32]{2,1,0:T(1,128)} %param.10) | copy-start | bytes 388
  94.1 72.6 %copy-start.4 = (f32[1,128]{1,0:T(1,128)S(1)}, f32[1,128]{1,0:T(1,128)}, u32[]{:S(2)}) copy-start(f32[1,128]{1,0:T(1,128)} %param.14) | copy-start | bytes 1540
Sparse Core Ops, SparseCore 0:
  10.1 80.5 all-gather.1
where the time goes:
time: 175 us
  blocking collectives  84.1 us (48%)
  waiting for transfers between devices  46.8 us (27%)
  matrix products  16.2 us (9%)
  between operations  15.5 us (9%)
  local copies, waits for them, and re-layouts  8.6 us (5%)
  other arithmetic  3.76 us (2%)
    unnamed x3, blocking collectives  57.6 us
    all_gather x1, waiting for transfers between devices, per_device(): lax.all_gather(history, ('col', 'lag'), axis=1, tiled=True)  46 us
    all_gather x1, blocking collectives, per_device(): lax.all_gather(history, ('row', 'lag'), axis=1, tiled=True)  26.4 us
    dot_general x1, matrix products, per_device(): jnp.einsum('plab,lpb,pl->pa', matrices, col_vectors, lag_mask, precision=...  10.1 us
    dot_general x1, matrix products, per_device(): jnp.einsum('plab,lpa,pl->pb', matrices, row_vectors, lag_mask, precision=...  4.16 us
    unnamed x13, local copies, waits for them, and re-layouts  3.91 us
  transfers between devices with their start and end apart: 1, of which 1 were waited for; matrix products, arithmetic and copies ran while one was open for 5% of the time, Pallas kernels for 0%

commit v1 on v0

v1 whole, which is shorter than its diff:
```python
import functools

import jax
import jax.numpy as jnp
from jax import lax
from jax.experimental import pallas as pl
from jax.experimental.pallas import tpu as pltpu
from jax.sharding import PartitionSpec as P

VMEM = pl.BlockSpec(memory_space=pltpu.VMEM)
SMEM = pl.BlockSpec(memory_space=pltpu.SMEM)


def order_kernel(lags, copies, step_ref, hist_ref, send_ref, past_ref):
    first = step_ref[0] - 1 + lags
    for g in range(lags):
        slot = lax.rem(first - g, lags)
        row = hist_ref[pl.ds(slot, 1), :]
        past_ref[pl.ds(g, 1), :] = row
        for k in range(copies):
            send_ref[pl.ds(k * lags + g, 1), :] = row


def forward_kernel(pairs, lag_local, n_lag, rows_ref, cols_ref, mask_ref, mats_ref, src_ref, past_ref, out_ref):
    lanes = lax.broadcasted_iota(jnp.int32, (128, 128), 1)

    def body(p, total):
        col = cols_ref[p]
        acc = jnp.zeros((128, 128), jnp.float32)
        for l in range(lag_local):
            keep = mask_ref[p, l] != 0
            vec = src_ref[pl.ds(col * lag_local + l, 1), :]
            acc = acc + mats_ref[p * lag_local + l] * jnp.where(keep, vec, 0.0)
        sums = jnp.sum(acc, axis=1, keepdims=True)
        return total + jnp.where(lanes == rows_ref[p], sums, 0.0)

    total = lax.fori_loop(0, pairs, body, jnp.zeros((128, 128), jnp.float32))
    chunk = lag_local + 1
    dests = out_ref.shape[0] // chunk
    out_ref[pl.ds(lag_local, dests, stride=chunk), :] = total.T[:dests]
    for d in range(dests):
        first = (d % n_lag) * lag_local
        out_ref[pl.ds(d * chunk, lag_local), :] = past_ref[pl.ds(first, lag_local), :]


def mirror_kernel(pairs, lag_local, n_lag, n_row, n_col, rows_ref, cols_ref, mask_ref, mats_ref, got_ref, out_ref, part_ref, held):
    chunk = lag_local + 1
    srcs = got_ref.shape[0] // chunk
    row_base = lax.axis_index("row") * (n_col * n_lag)
    col_base = lax.axis_index("col") * n_lag
    part_ref[...] = jnp.sum(got_ref[pl.ds(lag_local, srcs, stride=chunk), :], axis=0, keepdims=True)
    out_ref[...] = jnp.zeros(out_ref.shape, jnp.float32)
    for p in range(pairs):
        row = rows_ref[p]
        col = cols_ref[p]
        col_global = lax.div(col, n_lag) * (n_col * n_lag) + col_base + lax.rem(col, n_lag)
        off_diag = row_base + row != col_global
        for l in range(lag_local):
            keep = jnp.logical_and(mask_ref[p, l] != 0, off_diag)
            vec = got_ref[pl.ds(row * chunk + l, 1), :]
            held[pl.ds(p * lag_local + l, 1), :] = jnp.where(keep, vec, 0.0)
    turned = held[...].T

    def body(p, turned):
        acc = jnp.zeros((16, 8, 128), jnp.float32)
        for l in range(lag_local):
            acc = acc + (mats_ref[p * lag_local + l] * turned[:, l : l + 1]).reshape(16, 8, 128)
        total = jnp.sum(jnp.sum(acc, axis=0), axis=0, keepdims=True)
        at = pl.ds(cols_ref[p], 1)
        out_ref[at, :] = out_ref[at, :] + total
        return pltpu.roll(turned, 128 - lag_local, 1)

    lax.fori_loop(0, pairs, body, turned)


def final_kernel(got_ref, part_ref, incident_ref, inverse_ref, out_ref):
    convolved = jnp.sum(got_ref[...], axis=0, keepdims=True) + part_ref[...]
    rhs = incident_ref[...] - convolved
    sums = jnp.sum(inverse_ref[...] * rhs, axis=1, keepdims=True)
    out_ref[...] = jnp.broadcast_to(sums, (128, 128)).T[:1]


def per_device(n_row, n_col, n_lag, history, step_index, pair_rows, pair_cols, lag_pattern, blocks, incident, self_inverse):
    lags = history.shape[0]
    block = history.shape[2]
    pairs = blocks.shape[2]
    lag_local = blocks.shape[3]
    chunk = lag_local + 1
    f32 = jnp.float32
    rows = pair_rows.reshape(pairs)
    cols = pair_cols.reshape(pairs)
    mask = lag_pattern.reshape(pairs, lag_local)
    mats = blocks.reshape(pairs * lag_local, block, block)
    params = pltpu.CompilerParams(vmem_limit_bytes=16 * 1024 * 1024)

    send, past = pl.pallas_call(
        functools.partial(order_kernel, lags, n_row),
        out_shape=(
            jax.ShapeDtypeStruct((n_row * lags, block), f32),
            jax.ShapeDtypeStruct((lags, block), f32),
        ),
        in_specs=[SMEM, VMEM],
        out_specs=(VMEM, VMEM),
        name="order_lags",
    )(step_index, history.reshape(lags, block))
    send = send.reshape(n_row * n_lag, lag_local, block)
    col_source = lax.all_to_all(send, ("row", "lag"), 0, 0, tiled=True).reshape(n_row * lags, block)
    sent = pl.pallas_call(
        functools.partial(forward_kernel, pairs, lag_local, n_lag),
        out_shape=jax.ShapeDtypeStruct((n_col * n_lag * chunk, block), f32),
        in_specs=[SMEM, SMEM, SMEM, VMEM, VMEM, VMEM],
        out_specs=VMEM,
        name="forward",
        compiler_params=params,
    )(rows, cols, mask, mats, col_source, past)
    got = lax.all_to_all(
        sent.reshape(n_col * n_lag, chunk, 1, block), ("col", "lag"), 0, 0, tiled=True
    ).reshape(n_col * n_lag * chunk, block)
    mirrored, part = pl.pallas_call(
        functools.partial(mirror_kernel, pairs, lag_local, n_lag, n_row, n_col),
        out_shape=(
            jax.ShapeDtypeStruct((n_row * n_lag, block), f32),
            jax.ShapeDtypeStruct((1, block), f32),
        ),
        in_specs=[SMEM, SMEM, SMEM, VMEM, VMEM],
        out_specs=(VMEM, VMEM),
        scratch_shapes=[pltpu.VMEM((pairs * lag_local, block), f32)],
        name="mirror",
        compiler_params=params,
    )(rows, cols, mask, mats, got)
    fields = lax.all_to_all(
        mirrored.reshape(n_row * n_lag, 1, block), ("row", "lag"), 0, 0, tiled=True
    ).reshape(n_row * n_lag, block)
    return pl.pallas_call(
        final_kernel,
        out_shape=jax.ShapeDtypeStruct((1, block), f32),
        in_specs=[VMEM, VMEM, VMEM, VMEM],
        out_specs=VMEM,
        name="final",
    )(fields, part, incident, self_inverse.reshape(block, block))


def solution(mesh):
    in_specs = (
        P(None, ("row", "col", "lag"), None),
        P(),
        P("row", "col", None),
        P("row", "col", None),
        P("row", "col", None, "lag"),
        P("row", "col", None, "lag", None, None),
        P(("row", "col", "lag"), None),
        P(("row", "col", "lag"), None, None),
    )
    out_specs = P(("row", "col", "lag"), None)
    step = functools.partial(per_device, mesh.shape["row"], mesh.shape["col"], mesh.shape["lag"])
    return jax.shard_map(step, mesh=mesh, in_specs=in_specs, out_specs=out_specs, check_vma=False)
```

time: 175 us -> 68.3 us (0.39)
  blocking collectives: 84.1 us -> 32.3 us
  waiting for transfers between devices: 46.8 us -> 6.56 us
  matrix products: 16.2 us -> 0 us
  between operations: 15.5 us -> 0.72 us
  Pallas kernels: 0 us -> 13.5 us
  starting transfers between devices: 0.01 us -> 8.59 us
  other arithmetic: 3.76 us -> 0 us
  local copies, waits for them, and re-layouts: 8.6 us -> 6.19 us
    unnamed x3 -> x0, blocking collectives: 57.6 us -> none
    all_gather x1 -> x0, waiting for transfers between devices: 46 us -> none  [per_device(): lax.all_gather(history, ('col', 'lag'), axis=1, tiled=True)]
    all_to_all x0 -> x2, blocking collectives: none -> 32.3 us  [the longest x1 21.6 us: per_device(): lax.all_to_all(sent.reshape(n_col * n_lag, chunk, 1, block), ('col', 'lag...]
    all_gather x1 -> x0, blocking collectives: 26.4 us -> none  [per_device(): lax.all_gather(history, ('row', 'lag'), axis=1, tiled=True)]
    dot_general x5 -> x0, matrix products: 16.2 us -> none  [the longest x1 10.1 us: per_device(): jnp.einsum('plab,lpb,pl->pa', matrices, col_vectors, lag_mask, precision=...]
    pallas_call x0 -> x4, Pallas kernels: none -> 13.5 us  [the longest x1 6.33 us: per_device(): pl.pallas_call(functools.partial(mirror_kernel, pairs, lag_local, n_lag,...]
    all_to_all x0 -> x1, starting transfers between devices: none -> 8.59 us  [per_device(): lax.all_to_all(send, ('row', 'lag'), 0, 0, tiled=True)]
    all_to_all x0 -> x1, waiting for transfers between devices: none -> 6.56 us  [per_device(): lax.all_to_all(send, ('row', 'lag'), 0, 0, tiled=True)]
  transfers between devices with their start and end apart: 1 -> 1, of which waited for: 1 -> 1; matrix products, arithmetic and copies ran while one was open for 5% -> 1% of each run, Pallas kernels for 0% -> 0%
where the time goes in v1:
time: 68.3 us; the launch traced here: 67.8 us
  blocking collectives  32.3 us (47%)
  Pallas kernels  13.5 us (20%)
  starting transfers between devices  8.59 us (13%)
  waiting for transfers between devices  6.56 us (10%)
  local copies, waits for them, and re-layouts  6.19 us (9%)
  between operations  0.72 us (1%)
    all_to_all x1, blocking collectives, per_device(): lax.all_to_all(sent.reshape(n_col * n_lag, chunk, 1, block), ('col', 'lag...  21.6 us
    all_to_all x1, blocking collectives, per_device(): lax.all_to_all(mirrored.reshape(n_row * n_lag, 1, block), ('row', 'lag'),...  10.8 us
    all_to_all x1, starting transfers between devices, per_device(): lax.all_to_all(send, ('row', 'lag'), 0, 0, tiled=True)  8.59 us
    all_to_all x1, waiting for transfers between devices, per_device(): lax.all_to_all(send, ('row', 'lag'), 0, 0, tiled=True)  6.56 us
    pallas_call x1, Pallas kernels, per_device(): pl.pallas_call(functools.partial(mirror_kernel, pairs, lag_local, n_lag,...  6.33 us
    unnamed x16, local copies, waits for them, and re-layouts  5.42 us
    pallas_call x1, Pallas kernels, per_device(): pl.pallas_call(functools.partial(forward_kernel, pairs, lag_local, n_lag)...  4.16 us
    pallas_call x1, Pallas kernels, per_device(): pl.pallas_call(final_kernel, out_shape=jax.ShapeDtypeStruct((1, block), f...  1.54 us
  transfers between devices with their start and end apart: 1, of which 1 were waited for; matrix products, arithmetic and copies ran while one was open for 1% of the time, Pallas kernels for 0%

profile of v1, /device:TPU:1, one launch (start us, length us, event | category | flops | bytes accessed | tf_op | source)
XLA Modules:
  0.0 67.8 jit_solution(5027725017245261574)
XLA Ops:
  0.0 0.0 copy-start.6
  0.0 0.0 copy-start.4
  0.7 1.4 %order_lags.1 = (f32[128,128]{1,0:T(8,128)}, f32[32,128]{1,0:T(8,128)}) custom-call(s32[1]{0:T(128)S(6)} %copy.17.step_ref, f32[32,128]{1,0:T(8,128)} %bitcast.27), custom_call_target="tpu_custom_call" | custom-call | tf_op jit(solution)/shard_map/order_lags/pallas_call | solution.py:96
  2.1 8.6 %all-to-all-start = ((f32[32,4,128]{2,1,0:T(4,128)}), f32[32,4,128]{2,1,0:T(4,128)S(1)}, u32[]{:S(2)}, u32[]{:S(2)}) async-start(f32[32,4,128]{2,1,0:T(4,128)} %bitcast.25), calls=%async_computation | async-start | bytes 131072 | tf_op jit(solution)/shard_map/all_to_all | solution.py:107
  10.7 0.8 %copy.15.mask_ref = s32[32,4]{1,0:T(8,128)S(1)} copy(s32[32,4]{0,1:T(4,128)} %bitcast.28) | data formatting | bytes 1024 | tf_op jit(solution)/shard_map/reshape | solution.py:92
  11.5 6.6 %all-to-all-done = f32[32,4,128]{2,1,0:T(4,128)S(1)} async-done(((f32[32,4,128]{2,1,0:T(4,128)}), f32[32,4,128]{2,1,0:T(4,128)S(1)}, u32[]{:S(2)}, u32[]{:S(2)}) %all-to-all-start) | async-done | bytes 65568 | tf_op jit(solution)/shard_map/all_to_all | solution.py:107
  18.0 0.0 copy-start
  18.0 3.4 %copy-done = f32[1,1,32,4,128,128]{5,4,3,2,1,0:T(8,128)S(1)} copy-done((f32[1,1,32,4,128,128]{5,4,3,2,1,0:T(8,128)S(1)}, f32[1,1,32,4,128,128]{5,4,3,2,1,0:T(8,128)}, u32[]{:S(2)}) %copy-start) | copy-done | bytes 8388632
  21.4 0.0 copy-start.2
  21.4 0.7 %copy-done.2 = f32[32,128]{1,0:T(8,128)S(1)} copy-done((f32[32,128]{1,0:T(8,128)S(1)}, f32[32,128]{1,0:T(8,128)}, u32[]{:S(2)}) %copy-start.2) | copy-done | bytes 16408
  22.1 0.0 copy-start.3
  22.1 0.7 copy-done.3
  22.8 0.0 copy-start.5
  22.8 0.7 copy-done.5
  23.4 0.0 copy-start.1
  23.4 4.2 %forward.1 = f32[320,128]{1,0:T(8,128)S(1)} custom-call(s32[32]{0:T(128)S(1)} %bitcast.20, s32[32]{0:T(128)S(1)} %bitcast.22, s32[32,4]{1,0:T(8,128)S(1)} %copy.15.mask_ref, f32[128,128,128]{2,1,0:T(8,128)S(1)} %bitcast.14, f32[128,128]{1,0:T(8,128)S(1)} %bitcast.18, f32[32,128]{1,0:T(8,128)S(1)} %copy-done.2), custom_call_target="tpu_custom_call" | custom-call | tf_op jit(solution)/shard_map/forward/pallas_call | solution.py:108
  27.6 21.6 %all_to_all.15 = f32[64,5,1,128]{3,2,1,0:T(1,128)S(1)} all-to-all(f32[64,5,1,128]{3,2,1,0:T(1,128)S(1)} %bitcast.17), channel_id=1, replica_groups=mesh['row'=4,'col'=8,'lag'=8] {'col','lag'}, dimensions={0} | all-to-all | bytes 327680 | tf_op jit(solution)/shard_map/all_to_all | solution.py:116
  49.2 0.0 copy-done.6
  49.2 0.0 copy-done.4
  49.2 0.0 copy-done.1
  49.2 6.3 %mirror.1 = (f32[32,128]{1,0:T(8,128)S(1)}, f32[1,128]{1,0:T(1,128)S(1)}) custom-call(s32[32]{0:T(128)S(1)} %bitcast.21, s32[32]{0:T(128)S(1)} %bitcast.23, s32[32,4]{1,0:T(8,128)S(1)} %copy.15.mask_ref, f32[128,128,128]{2,1,0:T(8,128)S(1)} %bitcast.15, f32[320,128]{1,0:T(8,128)S(1)} %bitcast.16), custom_call_target="tpu_custom_call" | custom-call | tf_op jit(solution)/shard_map/mirror/pallas_call | solution.py:119
  55.5 0.0 copy-start.7
  55.5 10.8 %all_to_all.16 = f32[32,1,128]{2,1,0:T(1,128)} all-to-all(f32[32,1,128]{2,1,0:T(1,128)S(1)} %bitcast.19), channel_id=1, replica_groups=mesh['row'=4,'col'=8,'lag'=8] {'row','lag'}, dimensions={0} | all-to-all | bytes 32768 | tf_op jit(solution)/shard_map/all_to_all | solution.py:131
  66.3 0.0 copy-done.7
  66.3 1.5 %final.1 = f32[1,128]{1,0:T(1,128)} custom-call(f32[32,128]{1,0:T(8,128)} %bitcast.26, f32[1,128]{1,0:T(1,128)} %copy-done.7, f32[1,128]{1,0:T(1,128)} %incident_ref.1, f32[128,128]{1,0:T(8,128)} %bitcast.24), custom_call_target="tpu_custom_call" | custom-call | tf_op jit(solution)/shard_map/final/pallas_call | solution.py:134
Async XLA Ops:
  0.0 49.2 %copy-start.6 = (s32[1,1,32]{2,1,0:T(1,128)S(1)}, s32[1,1,32]{2,1,0:T(1,128)}, u32[]{:S(2)}) copy-start(s32[1,1,32]{2,1,0:T(1,128)} %param.11) | copy-start | bytes 388
  0.0 49.2 %copy-start.4 = (s32[1,1,32]{2,1,0:T(1,128)S(1)}, s32[1,1,32]{2,1,0:T(1,128)}, u32[]{:S(2)}) copy-start(s32[1,1,32]{2,1,0:T(1,128)} %param.10) | copy-start | bytes 388
  2.1 15.9 %all-to-all-start = ((f32[32,4,128]{2,1,0:T(4,128)}), f32[32,4,128]{2,1,0:T(4,128)S(1)}, u32[]{:S(2)}, u32[]{:S(2)}) async-start(f32[32,4,128]{2,1,0:T(4,128)} %bitcast.25), calls=%async_computation | async-start | bytes 131072 | tf_op jit(solution)/shard_map/all_to_all | solution.py:107
  18.0 3.4 %copy-start = (f32[1,1,32,4,128,128]{5,4,3,2,1,0:T(8,128)S(1)}, f32[1,1,32,4,128,128]{5,4,3,2,1,0:T(8,128)}, u32[]{:S(2)}) copy-start(f32[1,1,32,4,128,128]{5,4,3,2,1,0:T(8,128)} %param.13) | copy-start | bytes 25165828
  21.4 0.7 %copy-start.2 = (f32[32,128]{1,0:T(8,128)S(1)}, f32[32,128]{1,0:T(8,128)}, u32[]{:S(2)}) copy-start(f32[32,128]{1,0:T(8,128)} %get-tuple-element.10.past_ref) | copy-start | bytes 49156
  22.1 0.7 copy-start.3
  22.8 0.7 copy-start.5
  23.4 25.7 %copy-start.1 = (f32[1,1,32,4,128,128]{5,4,3,2,1,0:T(8,128)S(1)}, f32[1,1,32,4,128,128]{5,4,3,2,1,0:T(8,128)}, u32[]{:S(2)}) copy-start(f32[1,1,32,4,128,128]{5,4,3,2,1,0:T(8,128)} %param.13) | copy-start | bytes 25165828
  55.5 10.8 %copy-start.7 = (f32[1,128]{1,0:T(1,128)}, f32[1,128]{1,0:T(1,128)S(1)}, u32[]{:S(2)}) copy-start(f32[1,128]{1,0:T(1,128)S(1)} %get-tuple-element.12.part_ref) | copy-start | bytes 1540

commit v2 on v0

v2 whole, which is shorter than its diff:
```python
import functools

import jax
import jax.numpy as jnp
import numpy as np
from jax import lax
from jax.experimental import pallas as pl
from jax.experimental.pallas import tpu as pltpu
from jax.sharding import PartitionSpec as P

VMEM = pl.BlockSpec(memory_space=pltpu.VMEM)
F32 = jnp.float32
BF16 = jnp.bfloat16
MIB = 1024 * 1024
SIDE = 8
SPREAD = 3


def iota(shape, dim):
    return lax.broadcasted_iota(jnp.int32, shape, dim).astype(F32)


def split(values):
    high = values.astype(BF16)
    rest = values - high.astype(F32)
    mid = rest.astype(BF16)
    return high, mid, (rest - mid.astype(F32)).astype(BF16)


def select(picks, values):
    picks = picks.astype(BF16)
    high, mid, low = (jnp.dot(picks, part, preferred_element_type=F32) for part in split(values))
    return high + (mid + low)


def as_column(row, lanes):
    return jnp.broadcast_to(row, (lanes, row.shape[1])).T


def order_kernel(copies, step_ref, hist_ref, send_ref):
    lags = hist_ref.shape[0]
    slot = step_ref[...].astype(F32) - 1.0 - iota((lags, lags), 0)
    slot = jnp.where(slot < 0.0, slot + lags, slot)
    past = select(jnp.where(slot == iota((lags, lags), 1), 1.0, 0.0), hist_ref[...])
    for k in range(copies):
        send_ref[pl.ds(k * lags, lags), :] = past


def forward_kernel(n_col, n_lag, rows_ref, cols_ref, mask_ref, mats_ref, src_ref, out_ref, vecs):
    lag_local, pairs = mask_ref.shape
    terms = lag_local * pairs
    block = src_ref.shape[1]
    cols = cols_ref[...].astype(F32) * lag_local
    spots = [jnp.where(mask_ref[pl.ds(l, 1), :] != 0, cols + l, -1.0) for l in range(lag_local)]
    at = as_column(jnp.concatenate(spots, axis=1), block)
    vecs[...] = select(jnp.where(at == iota((terms, block), 1), 1.0, 0.0), src_ref[...])
    rows = as_column(rows_ref[...].astype(F32), block)
    hits = jnp.where(rows == iota((pairs, block), 1), 1.0, 0.0)
    total = jnp.zeros((block, block), F32)
    for p in range(pairs):
        acc = mats_ref[p * lag_local] * vecs[pl.ds(p, 1), :]
        for l in range(1, lag_local):
            acc = acc + mats_ref[p * lag_local + l] * vecs[pl.ds(l * pairs + p, 1), :]
        total = total + jnp.sum(acc, axis=1, keepdims=True) * hits[p : p + 1]
    fields = total.T
    own = n_lag * lag_local
    chunk = own + n_lag
    group = src_ref[pl.ds(pl.multiple_of(lax.axis_index("row") * own, own), own), :]
    for c in range(n_col):
        out_ref[pl.ds(c * chunk, own), :] = group
        out_ref[pl.ds(c * chunk + own, n_lag), :] = fields[c * n_lag : (c + 1) * n_lag]


def mirror_kernel(
    n_col, n_lag, rows_ref, cols_ref, mask_ref, mats_ref, got_ref, spread_ref, out_ref, sides, turned, held
):
    lag_local, pairs = mask_ref.shape
    block = got_ref.shape[1]
    terms = lag_local * pairs
    groups = pairs // SIDE
    per_group = SIDE * lag_local
    own = n_lag * lag_local
    chunk = own + n_lag
    row_index = lax.axis_index("row")
    row_base = (row_index * (n_col * n_lag)).astype(F32)
    col_base = (lax.axis_index("col") * n_lag).astype(F32)

    rows = rows_ref[...].astype(F32)
    cols = cols_ref[...].astype(F32)
    band = jnp.floor((cols + 0.5) * (1.0 / n_lag))
    col_global = band * (n_col * n_lag) + col_base + (cols - band * n_lag)
    off_diag = row_base + rows != col_global
    spots = [
        jnp.where(jnp.logical_and(mask_ref[pl.ds(l, 1), :] != 0, off_diag), rows * lag_local + l, -1.0)
        for l in range(lag_local)
    ]
    ordered = [spots[l][:, g * SIDE : (g + 1) * SIDE] for g in range(groups) for l in range(lag_local)]
    at = as_column(jnp.concatenate(ordered, axis=1), block)
    at = jnp.concatenate([at] * (n_col * own // block), axis=1)
    picks = jnp.where(at == iota(at.shape, 1), 1.0, 0.0)
    group_past = jnp.concatenate([got_ref[pl.ds(c * chunk, own), :] for c in range(n_col)], axis=0)
    columns = select(picks, group_past).T

    turned[...] = columns
    high = columns.astype(BF16).astype(F32)
    low = columns - high
    for g in range(groups):
        keep = slice(g * per_group, g * per_group + SPREAD * SIDE)
        sides[g] = jnp.concatenate([high[:, keep], low[:, keep]], axis=1).astype(BF16)
    for g in range(groups):
        side = sides[g]
        for q in range(SIDE):
            p = g * SIDE + q
            wide = jnp.dot(side, spread_ref[q], preferred_element_type=F32)
            acc = jnp.zeros((8, block), F32)
            for l in range(lag_local):
                if l < SPREAD:
                    factor = wide[:, l * block : (l + 1) * block]
                else:
                    lane = jnp.full((block, terms), g * per_group + l * SIDE + q, jnp.int32)
                    factor = jnp.take_along_axis(turned[...], lane, axis=1, mode="promise_in_bounds")
                product = mats_ref[p * lag_local + l] * factor
                acc = acc + jnp.sum(product.reshape(block // 8, 8, block), axis=0)
            held[pl.ds(p, 1), :] = jnp.sum(acc, axis=0, keepdims=True)

    dests = out_ref.shape[0]
    hits = jnp.where(cols == iota((dests, pairs), 0), 1.0, 0.0)
    out_ref[...] = select(hits, held[...])
    fields = got_ref[pl.ds(own, n_lag), :]
    for c in range(1, n_col):
        fields = fields + got_ref[pl.ds(c * chunk + own, n_lag), :]
    mine = pl.ds(pl.multiple_of(row_index * n_lag, n_lag), n_lag)
    out_ref[mine, :] = out_ref[mine, :] + fields


def final_kernel(got_ref, incident_ref, inverse_ref, out_ref):
    rhs = incident_ref[...] - jnp.sum(got_ref[...], axis=0, keepdims=True)
    sums = jnp.sum(inverse_ref[...] * rhs, axis=1, keepdims=True)
    out_ref[...] = jnp.broadcast_to(sums, inverse_ref.shape).T[:1]


def call(kernel, name, shape, operands, limit, scratch=()):
    return pl.pallas_call(
        kernel,
        out_shape=jax.ShapeDtypeStruct(shape, F32),
        in_specs=[VMEM] * len(operands),
        out_specs=VMEM,
        scratch_shapes=[pltpu.VMEM(*item) for item in scratch],
        name=name,
        compiler_params=pltpu.CompilerParams(vmem_limit_bytes=limit),
    )(*operands)


def spread_table(block):
    table = np.zeros((SIDE, 2, SPREAD, SIDE, SPREAD, block), np.float32)
    for q in range(SIDE):
        for l in range(SPREAD):
            table[q, :, l, q, l] = 1.0
    return table.reshape(SIDE, 2 * SPREAD * SIDE, SPREAD * block).astype(jnp.bfloat16)


def per_device(n_row, n_col, n_lag, history, step_index, pair_rows, pair_cols, lag_pattern, blocks, incident, self_inverse):
    lags = history.shape[0]
    block = history.shape[2]
    pairs = blocks.shape[2]
    lag_local = blocks.shape[3]
    terms = pairs * lag_local
    n_src = n_row * n_lag
    chunk = n_lag * lag_local + n_lag
    rows = pair_rows.reshape(1, pairs)
    cols = pair_cols.reshape(1, pairs)
    mask = lag_pattern.reshape(pairs, lag_local).T
    mats = blocks.reshape(terms, block, block)

    send = call(
        functools.partial(order_kernel, n_row),
        "order",
        (n_row * lags, block),
        [step_index.reshape(1, 1), history.reshape(lags, block)],
        MIB,
    )
    source = lax.all_to_all(
        send.reshape(n_src, lag_local, block), ("row", "lag"), 0, 0, tiled=True
    ).reshape(n_row * lags, block)
    sent = call(
        functools.partial(forward_kernel, n_col, n_lag),
        "forward",
        (n_col * chunk, block),
        [rows, cols, mask, mats, source],
        2 * MIB,
        [((terms, block), F32)],
    )
    got = lax.all_to_all(sent.reshape(n_col, chunk, block), "col", 0, 0, tiled=True)
    mirrored = call(
        functools.partial(mirror_kernel, n_col, n_lag),
        "mirror",
        (n_src, block),
        [rows, cols, mask, mats, got.reshape(n_col * chunk, block), spread_table(block)],
        3 * MIB,
        [
            ((pairs // SIDE, block, 2 * SPREAD * SIDE), BF16),
            ((block, terms), F32),
            ((pairs, block), F32),
        ],
    )
    fields = lax.all_to_all(mirrored.reshape(n_src, 1, block), ("row", "lag"), 0, 0, tiled=True)
    return call(
        final_kernel,
        "final",
        (1, block),
        [fields.reshape(n_src, block), incident, self_inverse.reshape(block, block)],
        MIB,
    )


def solution(mesh):
    in_specs = (
        P(None, ("row", "col", "lag"), None),
        P(),
        P("row", "col", None),
        P("row", "col", None),
        P("row", "col", None, "lag"),
        P("row", "col", None, "lag", None, None),
        P(("row", "col", "lag"), None),
        P(("row", "col", "lag"), None, None),
    )
    out_specs = P(("row", "col", "lag"), None)
    step = functools.partial(per_device, mesh.shape["row"], mesh.shape["col"], mesh.shape["lag"])
    return jax.shard_map(step, mesh=mesh, in_specs=in_specs, out_specs=out_specs, check_vma=False)
```

time: 175 us -> 55.6 us (0.32)
  waiting for transfers between devices: 46.8 us -> 0 us
  blocking collectives: 84.1 us -> 44.7 us
  matrix products: 16.2 us -> 0 us
  between operations: 15.5 us -> 0.74 us
  other arithmetic: 3.76 us -> 0 us
  Pallas kernels: 0 us -> 3.75 us
  local copies, waits for them, and re-layouts: 8.6 us -> 6.11 us
    unnamed x3 -> x0, blocking collectives: 57.6 us -> none
    all_gather x1 -> x0, waiting for transfers between devices: 46 us -> none  [per_device(): lax.all_gather(history, ('col', 'lag'), axis=1, tiled=True)]
    all_to_all x0 -> x3, blocking collectives: none -> 44.7 us  [the longest x1 16.8 us: per_device(): lax.all_to_all(sent.reshape(n_col, chunk, block), 'col', 0, 0, tiled=True)]
    all_gather x1 -> x0, blocking collectives: 26.4 us -> none  [per_device(): lax.all_gather(history, ('row', 'lag'), axis=1, tiled=True)]
    dot_general x5 -> x0, matrix products: 16.2 us -> none  [the longest x1 10.1 us: per_device(): jnp.einsum('plab,lpb,pl->pa', matrices, col_vectors, lag_mask, precision=...]
    pallas_call x0 -> x4, Pallas kernels: none -> 3.75 us  [call(): pl.pallas_call(kernel, out_shape=jax.ShapeDtypeStruct(shape, F32), in_spe...]
    gather x4 -> x0, local copies, waits for them, and re-layouts: 2.33 us -> none  [the longest x1 0.61 us: per_device(): row_vectors = jnp.take(row_source, rows_local, axis=1)]
    unnamed x13 -> x24, local copies, waits for them, and re-layouts: 3.91 us -> 6.11 us
  transfers between devices with their start and end apart: 1 -> 0, of which waited for: 1 -> 0; matrix products, arithmetic and copies ran while one was open for 5% -> 0% of each run, Pallas kernels for 0% -> 0%
where the time goes in v2:
time: 55.6 us; the launch traced here: 55.3 us
  blocking collectives  44.7 us (80%)
  local copies, waits for them, and re-layouts  6.11 us (11%)
  Pallas kernels  3.75 us (7%)
  between operations  0.74 us (1%)
    all_to_all x1, blocking collectives, per_device(): lax.all_to_all(sent.reshape(n_col, chunk, block), 'col', 0, 0, tiled=True)  16.8 us
    all_to_all x1, blocking collectives, per_device(): lax.all_to_all(send.reshape(n_src, lag_local, block), ('row', 'lag'), 0,...  15.7 us
    all_to_all x1, blocking collectives, per_device(): lax.all_to_all(mirrored.reshape(n_src, 1, block), ('row', 'lag'), 0, 0, t...  12.1 us
    unnamed x24, local copies, waits for them, and re-layouts  6.11 us
    pallas_call x4, Pallas kernels, call(): pl.pallas_call(kernel, out_shape=jax.ShapeDtypeStruct(shape, F32), in_spe...  3.75 us

profile of v2, /device:TPU:1, one launch (start us, length us, event | category | flops | bytes accessed | tf_op | source)
XLA Modules:
  0.0 55.3 jit_solution(5824515163184841664)
XLA Ops:
  0.0 0.0 copy-start.6
  0.0 0.0 copy-start.10
  0.0 0.0 copy-start.8
  0.7 0.0 copy-start.4
  0.7 0.7 %copy-done.4 = f32[32,1,128]{2,1,0:T(1,128)S(1)} copy-done((f32[32,1,128]{2,1,0:T(1,128)S(1)}, f32[32,1,128]{2,1,0:T(1,128)}, u32[]{:S(2)}) %copy-start.4) | copy-done | bytes 16408
  1.4 0.2 order.1
  1.6 15.7 %all_to_all.15 = f32[32,4,128]{2,1,0:T(4,128)S(1)} all-to-all(f32[32,4,128]{2,1,0:T(4,128)S(1)} %bitcast.23), channel_id=1, replica_groups=mesh['row'=4,'col'=8,'lag'=8] {'row','lag'}, dimensions={0} | all-to-all | bytes 131072 | tf_op jit(solution)/shard_map/all_to_all | solution.py:182
  17.3 0.0 copy-start
  17.3 3.4 %copy-done = f32[1,1,32,4,128,128]{5,4,3,2,1,0:T(8,128)S(1)} copy-done((f32[1,1,32,4,128,128]{5,4,3,2,1,0:T(8,128)S(1)}, f32[1,1,32,4,128,128]{5,4,3,2,1,0:T(8,128)}, u32[]{:S(2)}) %copy-start) | copy-done | bytes 8388632
  20.7 0.0 copy-start.5
  20.7 0.7 %copy-done.5 = s32[1,1,32,4]{2,3,1,0:T(4,128)S(1)} copy-done((s32[1,1,32,4]{2,3,1,0:T(4,128)S(1)}, s32[1,1,32,4]{2,3,1,0:T(4,128)}, u32[]{:S(2)}) %copy-start.5) | copy-done | bytes 536
  21.4 0.0 copy-start.7
  21.4 0.7 %copy-done.7 = s32[1,1,32]{2,1,0:T(1,128)S(1)} copy-done((s32[1,1,32]{2,1,0:T(1,128)S(1)}, s32[1,1,32]{2,1,0:T(1,128)}, u32[]{:S(2)}) %copy-start.7) | copy-done | bytes 152
  22.0 0.0 copy-start.9
  22.0 0.7 %copy-done.9 = s32[1,1,32]{2,1,0:T(1,128)S(1)} copy-done((s32[1,1,32]{2,1,0:T(1,128)S(1)}, s32[1,1,32]{2,1,0:T(1,128)}, u32[]{:S(2)}) %copy-start.9) | copy-done | bytes 152
  22.7 0.0 copy-start.1
  22.7 0.0 copy-start.2
  22.7 0.0 copy-start.3
  22.7 0.0 copy-start.11
  22.7 1.1 %forward.1 = f32[320,128]{1,0:T(8,128)S(1)} custom-call(s32[1,32]{1,0:T(1,128)S(1)} %bitcast.30, s32[1,32]{1,0:T(1,128)S(1)} %bitcast.32, s32[4,32]{1,0:T(4,128)S(1)} %bitcast.28, f32[128,128,128]{2,1,0:T(8,128)S(1)} %bitcast.18, f32[128,128]{1,0:T(8,128)S(1)} %bitcast.22), custom_call_target="tpu_custom_call" | custom-call | tf_op jit(solution)/shard_map/forward/pallas_call | solution.py:143
  23.9 16.8 %all_to_all.16 = f32[8,40,128]{2,1,0:T(8,128)S(1)} all-to-all(f32[8,40,128]{2,1,0:T(8,128)S(1)} %bitcast.21), channel_id=1, replica_groups=mesh['row'=4,'col'=8,'lag'=8] {'col'}, dimensions={0} | all-to-all | bytes 327680 | tf_op jit(solution)/shard_map/all_to_all | solution.py:193
  40.7 0.0 copy-done.6
  40.7 0.0 copy-done.10
  40.7 0.0 copy-done.8
  40.7 0.0 copy-done.1
  40.7 0.0 copy-done.2
  40.7 1.8 %mirror.1 = f32[32,128]{1,0:T(8,128)S(1)} custom-call(s32[1,32]{1,0:T(1,128)S(1)} %bitcast.31, s32[1,32]{1,0:T(1,128)S(1)} %bitcast.33, s32[4,32]{1,0:T(4,128)S(1)} %bitcast.29, f32[128,128,128]{2,1,0:T(8,128)S(1)} %bitcast.19, f32[320,128]{1,0:T(8,128)S(1)} %bitcast.20, bf16[8,48,384]{2,1,0:T(8,128)(2,1)S(1)} %copy-done.2), custom_call_target="tpu_custom_call" | custom-call | tf_op jit(solution)/shard_map/mirror/pallas_call | solution.py:143
  42.5 12.1 %all_to_all.17 = f32[32,1,128]{2,1,0:T(1,128)S(1)} all-to-all(f32[32,1,128]{2,1,0:T(1,128)S(1)} %bitcast.24), channel_id=1, replica_groups=mesh['row'=4,'col'=8,'lag'=8] {'row','lag'}, dimensions={0} | all-to-all | bytes 32768 | tf_op jit(solution)/shard_map/all_to_all | solution.py:206
  54.6 0.0 copy-done.3
  54.6 0.0 copy-done.11
  54.6 0.7 %final.1 = f32[1,128]{1,0:T(1,128)} custom-call(f32[32,128]{1,0:T(8,128)S(1)} %bitcast.26, f32[1,128]{1,0:T(1,128)S(1)} %copy-done.11, f32[128,128]{1,0:T(8,128)S(1)} %bitcast.25), custom_call_target="tpu_custom_call" | custom-call | tf_op jit(solution)/shard_map/final/pallas_call | solution.py:143
Async XLA Ops:
  0.0 40.7 %copy-start.6 = (s32[1,1,32,4]{2,3,1,0:T(4,128)S(1)}, s32[1,1,32,4]{2,3,1,0:T(4,128)}, u32[]{:S(2)}) copy-start(s32[1,1,32,4]{2,3,1,0:T(4,128)} %param.13) | copy-start | bytes 1540
  0.0 40.7 %copy-start.10 = (s32[1,1,32]{2,1,0:T(1,128)S(1)}, s32[1,1,32]{2,1,0:T(1,128)}, u32[]{:S(2)}) copy-start(s32[1,1,32]{2,1,0:T(1,128)} %param.12) | copy-start | bytes 388
  0.0 40.7 %copy-start.8 = (s32[1,1,32]{2,1,0:T(1,128)S(1)}, s32[1,1,32]{2,1,0:T(1,128)}, u32[]{:S(2)}) copy-start(s32[1,1,32]{2,1,0:T(1,128)} %param.11) | copy-start | bytes 388
  0.7 0.7 %copy-start.4 = (f32[32,1,128]{2,1,0:T(1,128)S(1)}, f32[32,1,128]{2,1,0:T(1,128)}, u32[]{:S(2)}) copy-start(f32[32,1,128]{2,1,0:T(1,128)} %param.9) | copy-start | bytes 49156
  17.3 3.4 %copy-start = (f32[1,1,32,4,128,128]{5,4,3,2,1,0:T(8,128)S(1)}, f32[1,1,32,4,128,128]{5,4,3,2,1,0:T(8,128)}, u32[]{:S(2)}) copy-start(f32[1,1,32,4,128,128]{5,4,3,2,1,0:T(8,128)} %param.14) | copy-start | bytes 25165828
  20.7 0.7 %copy-start.5 = (s32[1,1,32,4]{2,3,1,0:T(4,128)S(1)}, s32[1,1,32,4]{2,3,1,0:T(4,128)}, u32[]{:S(2)}) copy-start(s32[1,1,32,4]{2,3,1,0:T(4,128)} %param.13) | copy-start | bytes 1540
  21.4 0.7 %copy-start.7 = (s32[1,1,32]{2,1,0:T(1,128)S(1)}, s32[1,1,32]{2,1,0:T(1,128)}, u32[]{:S(2)}) copy-start(s32[1,1,32]{2,1,0:T(1,128)} %param.11) | copy-start | bytes 388
  22.0 0.7 %copy-start.9 = (s32[1,1,32]{2,1,0:T(1,128)S(1)}, s32[1,1,32]{2,1,0:T(1,128)}, u32[]{:S(2)}) copy-start(s32[1,1,32]{2,1,0:T(1,128)} %param.12) | copy-start | bytes 388
  22.7 18.0 %copy-start.1 = (f32[1,1,32,4,128,128]{5,4,3,2,1,0:T(8,128)S(1)}, f32[1,1,32,4,128,128]{5,4,3,2,1,0:T(8,128)}, u32[]{:S(2)}) copy-start(f32[1,1,32,4,128,128]{5,4,3,2,1,0:T(8,128)} %param.14) | copy-start | bytes 25165828
  22.7 18.0 %copy-start.2 = (bf16[8,48,384]{2,1,0:T(8,128)(2,1)S(1)}, bf16[8,48,384]{2,1,0:T(8,128)(2,1)}, u32[]{:S(2)}) copy-start(bf16[8,48,384]{2,1,0:T(8,128)(2,1)} %constant.2.clone.spread_ref) | copy-start | bytes 884740
  22.7 31.9 %copy-start.3 = (f32[1,128,128]{2,1,0:T(8,128)S(1)}, f32[1,128,128]{2,1,0:T(8,128)}, u32[]{:S(2)}) copy-start(f32[1,128,128]{2,1,0:T(8,128)} %param.16) | copy-start | bytes 196612
  22.7 31.9 %copy-start.11 = (f32[1,128]{1,0:T(1,128)S(1)}, f32[1,128]{1,0:T(1,128)}, u32[]{:S(2)}) copy-start(f32[1,128]{1,0:T(1,128)} %incident_ref.1) | copy-start | bytes 1540

commit v3 on v2

--- a/solution.py
+++ b/solution.py
@@ -148,6 +148,7 @@
         scratch_shapes=[pltpu.VMEM(*item) for item in scratch],
         name=name,
         compiler_params=pltpu.CompilerParams(vmem_limit_bytes=limit),
+        cost_estimate=pl.CostEstimate(flops=20_000_000_000, bytes_accessed=64 * MIB, transcendentals=0),
     )(*operands)
 
 

time: 55.6 us -> 50.1 us (0.901)
  local copies, waits for them, and re-layouts: 6.11 us -> 0.74 us
    unnamed x24 -> x16, local copies, waits for them, and re-layouts: 6.11 us -> 0.74 us
where the time goes in v3:
time: 50.1 us; the launch traced here: 49.9 us
  blocking collectives  44.7 us (89%)
  Pallas kernels  3.75 us (7%)
  local copies, waits for them, and re-layouts  0.74 us (1%)
  between operations  0.69 us (1%)
    all_to_all x1, blocking collectives, per_device(): lax.all_to_all(sent.reshape(n_col, chunk, block), 'col', 0, 0, tiled=True)  16.6 us
    all_to_all x1, blocking collectives, per_device(): lax.all_to_all(send.reshape(n_src, lag_local, block), ('row', 'lag'), 0,...  16 us
    all_to_all x1, blocking collectives, per_device(): lax.all_to_all(mirrored.reshape(n_src, 1, block), ('row', 'lag'), 0, 0, t...  12.1 us
    pallas_call x4, Pallas kernels, call(): pl.pallas_call(kernel, out_shape=jax.ShapeDtypeStruct(shape, F32), in_spe...  3.75 us

profile of v3, /device:TPU:1, one launch (start us, length us, event | category | flops | bytes accessed | tf_op | source)
XLA Modules:
  0.0 49.9 jit_solution(9474993880789970816)
XLA Ops:
  0.7 0.0 copy-start.2
  0.7 0.7 %copy-done.2 = f32[32,1,128]{2,1,0:T(1,128)S(1)} copy-done((f32[32,1,128]{2,1,0:T(1,128)S(1)}, f32[32,1,128]{2,1,0:T(1,128)}, u32[]{:S(2)}) %copy-start.2) | copy-done | bytes 16408
  1.4 0.0 copy-start
  1.4 0.0 copy-start.3
  1.4 0.0 copy-start.4
  1.4 0.0 copy-start.5
  1.4 0.2 order.1
  1.6 16.0 %all_to_all.15 = f32[32,4,128]{2,1,0:T(4,128)S(1)} all-to-all(f32[32,4,128]{2,1,0:T(4,128)S(1)} %bitcast.20), channel_id=1, replica_groups=mesh['row'=4,'col'=8,'lag'=8] {'row','lag'}, dimensions={0} | all-to-all | bytes 131072 | tf_op jit(solution)/shard_map/all_to_all | solution.py:183
  17.6 0.0 copy-done
  17.6 0.0 copy-done.3
  17.6 0.0 copy-done.4
  17.6 0.0 copy-done.5
  17.6 0.0 copy-start.7
  17.6 1.1 %forward.1 = f32[320,128]{1,0:T(8,128)S(1)} custom-call(s32[1,32]{1,0:T(1,128)S(1)} %bitcast.30, s32[1,32]{1,0:T(1,128)S(1)} %bitcast.32, s32[4,32]{1,0:T(4,128)S(1)} %bitcast.28, f32[128,128,128]{2,1,0:T(8,128)S(1)} %bitcast.24, f32[128,128]{1,0:T(8,128)S(1)} %bitcast.21), custom_call_target="tpu_custom_call" | custom-call | flops 20000000000 | bytes 67108864 | tf_op jit(solution)/shard_map/forward/pallas_call | solution.py:143
  18.7 16.6 %all_to_all.16 = f32[8,40,128]{2,1,0:T(8,128)S(1)} all-to-all(f32[8,40,128]{2,1,0:T(8,128)S(1)} %bitcast.19), channel_id=1, replica_groups=mesh['row'=4,'col'=8,'lag'=8] {'col'}, dimensions={0} | all-to-all | bytes 327680 | tf_op jit(solution)/shard_map/all_to_all | solution.py:194
  35.3 0.0 copy-done.7
  35.3 0.0 copy-start.1
  35.3 0.0 copy-start.6
  35.3 1.7 %mirror.1 = f32[32,128]{1,0:T(8,128)S(1)} custom-call(s32[1,32]{1,0:T(1,128)S(1)} %bitcast.31, s32[1,32]{1,0:T(1,128)S(1)} %bitcast.33, s32[4,32]{1,0:T(4,128)S(1)} %bitcast.29, f32[128,128,128]{2,1,0:T(8,128)S(1)} %bitcast.25, f32[320,128]{1,0:T(8,128)S(1)} %bitcast.18, bf16[8,48,384]{2,1,0:T(8,128)(2,1)S(1)} %copy-done.7), custom_call_target="tpu_custom_call" | custom-call | flops 20000000000 | bytes 67108864 | tf_op jit(solution)/shard_map/mirror/pallas_call | solution.py:143
  37.0 12.1 %all_to_all.17 = f32[32,1,128]{2,1,0:T(1,128)S(1)} all-to-all(f32[32,1,128]{2,1,0:T(1,128)S(1)} %bitcast.22), channel_id=1, replica_groups=mesh['row'=4,'col'=8,'lag'=8] {'row','lag'}, dimensions={0} | all-to-all | bytes 32768 | tf_op jit(solution)/shard_map/all_to_all | solution.py:207
  49.2 0.0 copy-done.1
  49.2 0.0 copy-done.6
  49.2 0.7 %final.1 = f32[1,128]{1,0:T(1,128)} custom-call(f32[32,128]{1,0:T(8,128)S(1)} %bitcast.23, f32[1,128]{1,0:T(1,128)S(1)} %copy-done.6, f32[128,128]{1,0:T(8,128)S(1)} %bitcast.26), custom_call_target="tpu_custom_call" | custom-call | flops 20000000000 | bytes 67108864 | tf_op jit(solution)/shard_map/final/pallas_call | solution.py:143
Async XLA Ops:
  0.7 0.7 %copy-start.2 = (f32[32,1,128]{2,1,0:T(1,128)S(1)}, f32[32,1,128]{2,1,0:T(1,128)}, u32[]{:S(2)}) copy-start(f32[32,1,128]{2,1,0:T(1,128)} %param.9) | copy-start | bytes 49156
  1.4 16.2 %copy-start = (f32[1,1,32,4,128,128]{5,4,3,2,1,0:T(8,128)S(1)}, f32[1,1,32,4,128,128]{5,4,3,2,1,0:T(8,128)}, u32[]{:S(2)}) copy-start(f32[1,1,32,4,128,128]{5,4,3,2,1,0:T(8,128)} %param.14) | copy-start | bytes 25165828
  1.4 16.2 %copy-start.3 = (s32[1,1,32,4]{2,3,1,0:T(4,128)S(1)}, s32[1,1,32,4]{2,3,1,0:T(4,128)}, u32[]{:S(2)}) copy-start(s32[1,1,32,4]{2,3,1,0:T(4,128)} %param.13) | copy-start | bytes 1540
  1.4 16.2 %copy-start.4 = (s32[1,1,32]{2,1,0:T(1,128)S(1)}, s32[1,1,32]{2,1,0:T(1,128)}, u32[]{:S(2)}) copy-start(s32[1,1,32]{2,1,0:T(1,128)} %param.11) | copy-start | bytes 388
  1.4 16.2 %copy-start.5 = (s32[1,1,32]{2,1,0:T(1,128)S(1)}, s32[1,1,32]{2,1,0:T(1,128)}, u32[]{:S(2)}) copy-start(s32[1,1,32]{2,1,0:T(1,128)} %param.12) | copy-start | bytes 388
  17.6 17.7 %copy-start.7 = (bf16[8,48,384]{2,1,0:T(8,128)(2,1)S(1)}, bf16[8,48,384]{2,1,0:T(8,128)(2,1)}, u32[]{:S(2)}) copy-start(bf16[8,48,384]{2,1,0:T(8,128)(2,1)} %constant.2.clone.spread_ref) | copy-start | bytes 884740
  35.3 13.9 %copy-start.1 = (f32[1,128,128]{2,1,0:T(8,128)S(1)}, f32[1,128,128]{2,1,0:T(8,128)}, u32[]{:S(2)}) copy-start(f32[1,128,128]{2,1,0:T(8,128)} %param.16) | copy-start | bytes 196612
  35.3 13.9 %copy-start.6 = (f32[1,128]{1,0:T(1,128)S(1)}, f32[1,128]{1,0:T(1,128)}, u32[]{:S(2)}) copy-start(f32[1,128]{1,0:T(1,128)} %incident_ref.1) | copy-start | bytes 1540

commit v4 on v3

v4 whole, which is shorter than its diff:
```python
import functools

import jax
import jax.numpy as jnp
from jax import lax
from jax.experimental import pallas as pl
from jax.experimental.pallas import tpu as pltpu
from jax.sharding import PartitionSpec as P

VMEM = pl.BlockSpec(memory_space=pltpu.VMEM)
F32 = jnp.float32
BF16 = jnp.bfloat16
MIB = 1024 * 1024
SIDE = 8
SPREAD = 3
TOGETHER = 2


def iota(shape, dim):
    return lax.broadcasted_iota(jnp.int32, shape, dim).astype(F32)


def split(values):
    high = values.astype(BF16)
    rest = values - high.astype(F32)
    mid = rest.astype(BF16)
    return high, mid, (rest - mid.astype(F32)).astype(BF16)


def select(picks, values):
    picks = picks.astype(BF16)
    return jnp.dot(
        jnp.concatenate([picks] * 3, axis=1), jnp.concatenate(split(values), axis=0), preferred_element_type=F32
    )


def as_column(row, lanes):
    return jnp.broadcast_to(row, (lanes, row.shape[1])).T


def pick_rows(spots, width):
    at = as_column(spots, 128)
    at = jnp.concatenate([at] * (width // 128), axis=1)
    return jnp.where(at == iota(at.shape, 1), 1.0, 0.0).astype(BF16)


def table_kernel(spread_ref, token_ref):
    batches, height, width = spread_ref.shape
    source = lax.broadcasted_iota(jnp.int32, (height, width), 0)
    target = lax.broadcasted_iota(jnp.int32, (height, width), 1)
    token_ref[...] = jnp.zeros(token_ref.shape, F32)
    for batch in range(batches):
        table = jnp.zeros((height, width), F32)
        for t in range(TOGETHER):
            for l in range(SPREAD):
                first = (t * SPREAD + l) * 128
                lanes = jnp.logical_and(target >= first, target < first + 128)
                row = l * SIDE + batch * TOGETHER + t
                rows = jnp.logical_or(source == row, source == row + SPREAD * SIDE)
                table = jnp.where(jnp.logical_and(lanes, rows), 1.0, table)
        spread_ref[batch] = table.astype(BF16)


def order_kernel(
    copies, step_ref, hist_ref, rows_ref, cols_ref, mask_ref, token_ref, send_ref, picks_ref, hits_ref
):
    del token_ref
    lags = hist_ref.shape[0]
    slot = step_ref[...].astype(F32) - 1.0 - iota((lags, lags), 0)
    slot = jnp.where(slot < 0.0, slot + lags, slot)
    turn = jnp.where(slot == iota((lags, lags), 1), 1.0, 0.0).astype(BF16)
    high, mid, low = (jnp.dot(turn, part, preferred_element_type=F32) for part in split(hist_ref[...]))
    past = high + (mid + low)
    for k in range(copies):
        send_ref[pl.ds(k * lags, lags), :] = past

    lag_local = mask_ref.shape[0]
    cols = cols_ref[...].astype(F32) * lag_local
    spots = [jnp.where(mask_ref[pl.ds(l, 1), :] != 0, cols + l, -1.0) for l in range(lag_local)]
    picks_ref[...] = pick_rows(jnp.concatenate(spots, axis=1), picks_ref.shape[1])
    rows = as_column(rows_ref[...].astype(F32), hits_ref.shape[1])
    hits_ref[...] = jnp.where(rows == iota(hits_ref.shape, 1), 1.0, 0.0)


def forward_kernel(
    n_col, n_lag, rows_ref, cols_ref, mask_ref, mats_ref, src_ref, picks_ref, hits_ref,
    out_ref, mirror_picks_ref, mirror_hits_ref, vecs,
):
    lag_local, pairs = mask_ref.shape
    block = src_ref.shape[1]
    own = n_lag * lag_local
    chunk = own + n_lag
    vecs[...] = select(picks_ref[...], src_ref[...])
    group = src_ref[pl.ds(pl.multiple_of(lax.axis_index("row") * own, own), own), :]
    total = jnp.zeros((block, block), F32)
    for p in range(pairs):
        acc = mats_ref[p * lag_local] * vecs[pl.ds(p, 1), :]
        for l in range(1, lag_local):
            acc = acc + mats_ref[p * lag_local + l] * vecs[pl.ds(l * pairs + p, 1), :]
        total = total + jnp.sum(acc, axis=1, keepdims=True) * hits_ref[pl.ds(p, 1), :]
    fields = total.T
    for c in range(n_col):
        out_ref[pl.ds(c * chunk, own), :] = group
        out_ref[pl.ds(c * chunk + own, n_lag), :] = fields[c * n_lag : (c + 1) * n_lag]

    row_base = (lax.axis_index("row") * (n_col * n_lag)).astype(F32)
    col_base = (lax.axis_index("col") * n_lag).astype(F32)
    rows = rows_ref[...].astype(F32)
    cols = cols_ref[...].astype(F32)
    band = jnp.floor((cols + 0.5) * (1.0 / n_lag))
    col_global = band * (n_col * n_lag) + col_base + (cols - band * n_lag)
    off_diag = row_base + rows != col_global
    spots = [
        jnp.where(jnp.logical_and(mask_ref[pl.ds(l, 1), :] != 0, off_diag), rows * lag_local + l, -1.0)
        for l in range(lag_local)
    ]
    ordered = [
        spots[l][:, g * SIDE : (g + 1) * SIDE] for g in range(pairs // SIDE) for l in range(lag_local)
    ]
    mirror_picks_ref[...] = pick_rows(jnp.concatenate(ordered, axis=1), mirror_picks_ref.shape[1])
    cols = jnp.concatenate([cols] * 8, axis=1)
    mirror_hits_ref[...] = jnp.where(cols == iota(mirror_hits_ref.shape, 0), 1.0, 0.0).astype(BF16)


def mirror_kernel(
    n_col, n_lag, lag_local, mats_ref, got_ref, picks_ref, hits_ref, spread_ref, out_ref, sides, turned, held
):
    pairs = hits_ref.shape[1] // 8
    block = got_ref.shape[1]
    terms = lag_local * pairs
    groups = pairs // SIDE
    per_group = SIDE * lag_local
    own = n_lag * lag_local
    chunk = own + n_lag
    group_past = jnp.concatenate([got_ref[pl.ds(c * chunk, own), :] for c in range(n_col)], axis=0)
    columns = select(picks_ref[...], group_past).T
    turned[...] = columns
    high = columns.astype(BF16).astype(F32)
    low = columns - high
    for g in range(groups):
        keep = slice(g * per_group, g * per_group + SPREAD * SIDE)
        sides[g] = jnp.concatenate([high[:, keep], low[:, keep]], axis=1).astype(BF16)
    for g in range(groups):
        side = sides[g]
        for q in range(0, SIDE, TOGETHER):
            wide = jnp.dot(side, spread_ref[q // TOGETHER], preferred_element_type=F32)
            for t in range(TOGETHER):
                p = g * SIDE + q + t
                acc = jnp.zeros((8, block), F32)
                for l in range(lag_local):
                    if l < SPREAD:
                        first = (t * SPREAD + l) * block
                        factor = wide[:, first : first + block]
                    else:
                        lane = jnp.full((block, terms), g * per_group + l * SIDE + q + t, jnp.int32)
                        factor = jnp.take_along_axis(turned[...], lane, axis=1, mode="promise_in_bounds")
                    product = mats_ref[p * lag_local + l] * factor
                    acc = acc + jnp.sum(product.reshape(block // 8, 8, block), axis=0)
                held[pl.ds(p, 8, stride=pairs), :] = acc

    out_ref[...] = select(hits_ref[...], held[...])
    fields = got_ref[pl.ds(own, n_lag), :]
    for c in range(1, n_col):
        fields = fields + got_ref[pl.ds(c * chunk + own, n_lag), :]
    mine = pl.ds(pl.multiple_of(lax.axis_index("row") * n_lag, n_lag), n_lag)
    out_ref[mine, :] = out_ref[mine, :] + fields


def final_kernel(got_ref, incident_ref, inverse_ref, out_ref):
    rhs = incident_ref[...] - jnp.sum(got_ref[...], axis=0, keepdims=True)
    sums = jnp.sum(inverse_ref[...] * rhs, axis=1, keepdims=True)
    out_ref[...] = jnp.broadcast_to(sums, inverse_ref.shape).T[:1]


def call(kernel, name, outs, operands, limit, scratch=()):
    return pl.pallas_call(
        kernel,
        out_shape=tuple(jax.ShapeDtypeStruct(*out) for out in outs),
        in_specs=[VMEM] * len(operands),
        out_specs=tuple(VMEM for _ in outs),
        scratch_shapes=[pltpu.VMEM(*item) for item in scratch],
        name=name,
        compiler_params=pltpu.CompilerParams(vmem_limit_bytes=limit),
        cost_estimate=pl.CostEstimate(flops=20_000_000_000, bytes_accessed=64 * MIB, transcendentals=0),
    )(*operands)


def per_device(n_row, n_col, n_lag, history, step_index, pair_rows, pair_cols, lag_pattern, blocks, incident, self_inverse):
    lags = history.shape[0]
    block = history.shape[2]
    pairs = blocks.shape[2]
    lag_local = blocks.shape[3]
    terms = pairs * lag_local
    n_src = n_row * n_lag
    own = n_lag * lag_local
    chunk = own + n_lag
    rows = pair_rows.reshape(1, pairs)
    cols = pair_cols.reshape(1, pairs)
    mask = lag_pattern.reshape(pairs, lag_local).T
    mats = blocks.reshape(terms, block, block)

    spread, token = call(
        table_kernel,
        "table",
        [((SIDE // TOGETHER, 2 * SPREAD * SIDE, TOGETHER * SPREAD * block), BF16), ((8, block), F32)],
        [],
        MIB,
    )
    send, picks, hits = call(
        functools.partial(order_kernel, n_row),
        "order",
        [((n_row * lags, block), F32), ((terms, n_row * lags), BF16), ((pairs, block), F32)],
        [step_index.reshape(1, 1), history.reshape(lags, block), rows, cols, mask, token],
        MIB,
    )
    source = lax.all_to_all(
        send.reshape(n_src, lag_local, block), ("row", "lag"), 0, 0, tiled=True
    ).reshape(n_row * lags, block)
    sent, mirror_picks, mirror_hits = call(
        functools.partial(forward_kernel, n_col, n_lag),
        "forward",
        [((n_col * chunk, block), F32), ((terms, n_col * own), BF16), ((n_src, 8 * pairs), BF16)],
        [rows, cols, mask, mats, source, picks, hits],
        2 * MIB,
        [((terms, block), F32)],
    )
    got = lax.all_to_all(sent.reshape(n_col, chunk, block), "col", 0, 0, tiled=True)
    (mirrored,) = call(
        functools.partial(mirror_kernel, n_col, n_lag, lag_local),
        "mirror",
        [((n_src, block), F32)],
        [mats, got.reshape(n_col * chunk, block), mirror_picks, mirror_hits, spread],
        3 * MIB,
        [
            ((pairs // SIDE, block, 2 * SPREAD * SIDE), BF16),
            ((block, terms), F32),
            ((8 * pairs, block), F32),
        ],
    )
    fields = lax.all_to_all(mirrored.reshape(n_src, 1, block), ("row", "lag"), 0, 0, tiled=True)
    return call(
        final_kernel,
        "final",
        [((1, block), F32)],
        [fields.reshape(n_src, block), incident, self_inverse.reshape(block, block)],
        MIB,
    )[0]


def solution(mesh):
    in_specs = (
        P(None, ("row", "col", "lag"), None),
        P(),
        P("row", "col", None),
        P("row", "col", None),
        P("row", "col", None, "lag"),
        P("row", "col", None, "lag", None, None),
        P(("row", "col", "lag"), None),
        P(("row", "col", "lag"), None, None),
    )
    out_specs = P(("row", "col", "lag"), None)
    step = functools.partial(per_device, mesh.shape["row"], mesh.shape["col"], mesh.shape["lag"])
    return jax.shard_map(step, mesh=mesh, in_specs=in_specs, out_specs=out_specs, check_vma=False)
```

time: 50.1 us -> 49.2 us (0.982)
  local copies, waits for them, and re-layouts: 0.74 us -> 0.04 us
    unnamed x16, local copies, waits for them, and re-layouts: 0.74 us -> 0.04 us
    pallas_call x4 -> x5, Pallas kernels: 3.75 us -> 3.39 us  [call(): pl.pallas_call(kernel, out_shape=tuple((jax.ShapeDtypeStruct(*out) for ou...]
where the time goes in v4:
time: 49.2 us; the launch traced here: 49 us
  blocking collectives  44.7 us (91%)
  Pallas kernels  3.39 us (7%)
  between operations  0.88 us (2%)
    all_to_all x1, blocking collectives, per_device(): lax.all_to_all(sent.reshape(n_col, chunk, block), 'col', 0, 0, tiled=True)  16.6 us
    all_to_all x1, blocking collectives, per_device(): lax.all_to_all(send.reshape(n_src, lag_local, block), ('row', 'lag'), 0,...  16 us
    all_to_all x1, blocking collectives, per_device(): lax.all_to_all(mirrored.reshape(n_src, 1, block), ('row', 'lag'), 0, 0, t...  12.2 us
    pallas_call x5, Pallas kernels, call(): pl.pallas_call(kernel, out_shape=tuple((jax.ShapeDtypeStruct(*out) for ou...  3.39 us

profile of v4, /device:TPU:1, one launch (start us, length us, event | category | flops | bytes accessed | tf_op | source)
XLA Modules:
  0.0 49.0 jit_solution(6924753872656434652)
XLA Ops:
  0.0 0.0 copy-start.2
  0.0 0.0 copy-start.4
  0.0 0.0 copy-start.3
  0.0 0.0 copy-start.1
  0.0 0.0 slice-start
  0.9 0.0 copy-done.2
  0.9 0.0 copy-done.4
  0.9 0.0 copy-done.3
  0.9 0.0 copy-done.1
  0.9 0.0 slice-start.1
  0.9 0.2 order.1
  1.1 16.0 %all_to_all.15 = f32[32,4,128]{2,1,0:T(4,128)S(1)} all-to-all(f32[32,4,128]{2,1,0:T(4,128)S(1)} %bitcast.21), channel_id=1, replica_groups=mesh['row'=4,'col'=8,'lag'=8] {'row','lag'}, dimensions={0} | all-to-all | bytes 131072 | tf_op jit(solution)/shard_map/all_to_all | solution.py:216
  17.1 0.0 slice-done
  17.1 0.0 slice-done.1
  17.1 1.0 %forward.1 = (f32[320,128]{1,0:T(8,128)S(1)}, bf16[128,256]{1,0:T(8,128)(2,1)S(1)}, bf16[32,256]{1,0:T(8,128)(2,1)S(1)}) custom-call(s32[1,32]{1,0:T(1,128)S(1)} %bitcast.33, s32[1,32]{1,0:T(1,128)S(1)} %bitcast.35, s32[4,32]{1,0:T(4,128)S(1)} %bitcast.31, f32[128,128,128]{2,1,0:T(8,128)S(1)} %bitcast.26, f32[128,128]{1,0:T(8,128)S(1)} %bitcast.20, ...), custom_call_target="tpu_custom_call" | custom-call | flops 20000000000 | bytes 67108864 | tf_op jit(solution)/shard_map/forward/pallas_call | solution.py:176
  18.1 16.6 %all_to_all.16 = f32[8,40,128]{2,1,0:T(8,128)S(1)} all-to-all(f32[8,40,128]{2,1,0:T(8,128)S(1)} %bitcast.18), channel_id=1, replica_groups=mesh['row'=4,'col'=8,'lag'=8] {'col'}, dimensions={0} | all-to-all | bytes 327680 | tf_op jit(solution)/shard_map/all_to_all | solution.py:227
  34.7 0.0 copy-start
  34.7 0.0 copy-start.5
  34.7 1.5 %mirror.1 = f32[32,128]{1,0:T(8,128)S(1)} custom-call(f32[128,128,128]{2,1,0:T(8,128)S(1)} %bitcast.27, f32[320,128]{1,0:T(8,128)S(1)} %bitcast.19, bf16[128,256]{1,0:T(8,128)(2,1)S(1)} %get-tuple-element.18.picks_ref, bf16[32,256]{1,0:T(8,128)(2,1)S(1)} %get-tuple-element.19.hits_ref, bf16[4,48,768]{2,1,0:T(8,128)(2,1)S(1)} %get-tuple-element.20.spread_ref), custom_call_target="tpu_custom_call" | custom-call | flops 20000000000 | bytes 67108864 | tf_op jit(solution)/shard_map/mirror/pallas_call | solution.py:176
  36.2 12.2 %all_to_all.17 = f32[32,1,128]{2,1,0:T(1,128)S(1)} all-to-all(f32[32,1,128]{2,1,0:T(1,128)S(1)} %bitcast.22), channel_id=1, replica_groups=mesh['row'=4,'col'=8,'lag'=8] {'row','lag'}, dimensions={0} | all-to-all | bytes 32768 | tf_op jit(solution)/shard_map/all_to_all | solution.py:240
  48.3 0.0 copy-done
  48.3 0.0 copy-done.5
  48.3 0.7 %final.1 = f32[1,128]{1,0:T(1,128)} custom-call(f32[32,128]{1,0:T(8,128)S(1)} %bitcast.23, f32[1,128]{1,0:T(1,128)S(1)} %copy-done.5, f32[128,128]{1,0:T(8,128)S(1)} %bitcast.28), custom_call_target="tpu_custom_call" | custom-call | flops 20000000000 | bytes 67108864 | tf_op jit(solution)/shard_map/final/pallas_call | solution.py:176
  (2 shorter events, 0.0 us)
Async XLA Ops:
  0.0 0.9 %copy-start.2 = (s32[1,1,32,4]{2,3,1,0:T(4,128)S(1)}, s32[1,1,32,4]{2,3,1,0:T(4,128)}, u32[]{:S(2)}) copy-start(s32[1,1,32,4]{2,3,1,0:T(4,128)} %param.12) | copy-start | bytes 1540
  0.0 0.9 %copy-start.4 = (s32[1,1,32]{2,1,0:T(1,128)S(1)}, s32[1,1,32]{2,1,0:T(1,128)}, u32[]{:S(2)}) copy-start(s32[1,1,32]{2,1,0:T(1,128)} %param.11) | copy-start | bytes 388
  0.0 0.9 %copy-start.3 = (s32[1,1,32]{2,1,0:T(1,128)S(1)}, s32[1,1,32]{2,1,0:T(1,128)}, u32[]{:S(2)}) copy-start(s32[1,1,32]{2,1,0:T(1,128)} %param.10) | copy-start | bytes 388
  0.0 0.9 %copy-start.1 = (f32[32,1,128]{2,1,0:T(1,128)S(1)}, f32[32,1,128]{2,1,0:T(1,128)}, u32[]{:S(2)}) copy-start(f32[32,1,128]{2,1,0:T(1,128)} %param.8) | copy-start | bytes 49156
  0.0 17.1 %slice-start = ((s8[8388608]{0:T(1024)(128)(4,1)}), s8[4194304]{0:T(1024)(128)(4,1)S(1)}, s32[]{:S(2)}) async-start(s8[8388608]{0:T(1024)(128)(4,1)} %bitcast.24), calls=%async_computation.3 | async-start | bytes 8388608
  0.9 16.2 %slice-start.1 = ((s8[8388608]{0:T(1024)(128)(4,1)}), s8[4194304]{0:T(1024)(128)(4,1)S(1)}, s32[]{:S(2)}) async-start(s8[8388608]{0:T(1024)(128)(4,1)} %bitcast.24), calls=%async_computation.4 | async-start | bytes 8388608
  34.7 13.6 %copy-start = (f32[1,128,128]{2,1,0:T(8,128)S(1)}, f32[1,128,128]{2,1,0:T(8,128)}, u32[]{:S(2)}) copy-start(f32[1,128,128]{2,1,0:T(8,128)} %param.15) | copy-start | bytes 196612
  34.7 13.6 %copy-start.5 = (f32[1,128]{1,0:T(1,128)S(1)}, f32[1,128]{1,0:T(1,128)}, u32[]{:S(2)}) copy-start(f32[1,128]{1,0:T(1,128)} %incident_ref.1) | copy-start | bytes 1540

commit v5 on v4

--- a/solution.py
+++ b/solution.py
@@ -14,23 +14,24 @@
 SIDE = 8
 SPREAD = 3
 TOGETHER = 2
+COL_ORDER = (5, 4, 6, 3, 7, 2, 0, 1)
 
 
 def iota(shape, dim):
     return lax.broadcasted_iota(jnp.int32, shape, dim).astype(F32)
 
 
-def split(values):
-    high = values.astype(BF16)
-    rest = values - high.astype(F32)
-    mid = rest.astype(BF16)
-    return high, mid, (rest - mid.astype(F32)).astype(BF16)
+def split(values, parts):
+    pieces = []
+    for _ in range(parts - 1):
+        pieces.append(values.astype(BF16))
+        values = values - pieces[-1].astype(F32)
+    return pieces + [values.astype(BF16)]
 
 
 def select(picks, values):
-    picks = picks.astype(BF16)
     return jnp.dot(
-        jnp.concatenate([picks] * 3, axis=1), jnp.concatenate(split(values), axis=0), preferred_element_type=F32
+        jnp.concatenate([picks] * 2, axis=1), jnp.concatenate(split(values, 2), axis=0), preferred_element_type=F32
     )
 
 
@@ -61,15 +62,25 @@
         spread_ref[batch] = table.astype(BF16)
 
 
+def turned(index, size, first):
+    index = index - first
+    return jnp.where(index < 0.0, index + size, index)
+
+
+def parts_of(index, size):
+    major = jnp.floor((index + 0.5) * (1.0 / size))
+    return major, index - major * size
+
+
 def order_kernel(
-    copies, step_ref, hist_ref, rows_ref, cols_ref, mask_ref, token_ref, send_ref, picks_ref, hits_ref
+    n_lag, copies, step_ref, hist_ref, rows_ref, cols_ref, mask_ref, token_ref, send_ref, picks_ref, hits_ref
 ):
     del token_ref
     lags = hist_ref.shape[0]
     slot = step_ref[...].astype(F32) - 1.0 - iota((lags, lags), 0)
     slot = jnp.where(slot < 0.0, slot + lags, slot)
     turn = jnp.where(slot == iota((lags, lags), 1), 1.0, 0.0).astype(BF16)
-    high, mid, low = (jnp.dot(turn, part, preferred_element_type=F32) for part in split(hist_ref[...]))
+    high, mid, low = (jnp.dot(turn, part, preferred_element_type=F32) for part in split(hist_ref[...], 3))
     past = high + (mid + low)
     for k in range(copies):
         send_ref[pl.ds(k * lags, lags), :] = past
@@ -78,12 +89,13 @@
     cols = cols_ref[...].astype(F32) * lag_local
     spots = [jnp.where(mask_ref[pl.ds(l, 1), :] != 0, cols + l, -1.0) for l in range(lag_local)]
     picks_ref[...] = pick_rows(jnp.concatenate(spots, axis=1), picks_ref.shape[1])
-    rows = as_column(rows_ref[...].astype(F32), hits_ref.shape[1])
+    major, minor = parts_of(rows_ref[...].astype(F32), n_lag)
+    rows = as_column(major * n_lag + turned(minor, n_lag, n_lag // 2), hits_ref.shape[1])
     hits_ref[...] = jnp.where(rows == iota(hits_ref.shape, 1), 1.0, 0.0)
 
 
 def forward_kernel(
-    n_col, n_lag, rows_ref, cols_ref, mask_ref, mats_ref, src_ref, picks_ref, hits_ref,
+    n_row, n_col, n_lag, rows_ref, cols_ref, mask_ref, mats_ref, src_ref, picks_ref, hits_ref,
     out_ref, mirror_picks_ref, mirror_hits_ref, vecs,
 ):
     lag_local, pairs = mask_ref.shape
@@ -100,15 +112,16 @@
         total = total + jnp.sum(acc, axis=1, keepdims=True) * hits_ref[pl.ds(p, 1), :]
     fields = total.T
     for c in range(n_col):
-        out_ref[pl.ds(c * chunk, own), :] = group
-        out_ref[pl.ds(c * chunk + own, n_lag), :] = fields[c * n_lag : (c + 1) * n_lag]
+        at = COL_ORDER.index(c) * chunk
+        out_ref[pl.ds(at, own), :] = group
+        out_ref[pl.ds(at + own, n_lag), :] = fields[c * n_lag : (c + 1) * n_lag]
 
     row_base = (lax.axis_index("row") * (n_col * n_lag)).astype(F32)
     col_base = (lax.axis_index("col") * n_lag).astype(F32)
     rows = rows_ref[...].astype(F32)
     cols = cols_ref[...].astype(F32)
-    band = jnp.floor((cols + 0.5) * (1.0 / n_lag))
-    col_global = band * (n_col * n_lag) + col_base + (cols - band * n_lag)
+    band, inner = parts_of(cols, n_lag)
+    col_global = band * (n_col * n_lag) + col_base + inner
     off_diag = row_base + rows != col_global
     spots = [
         jnp.where(jnp.logical_and(mask_ref[pl.ds(l, 1), :] != 0, off_diag), rows * lag_local + l, -1.0)
@@ -118,12 +131,13 @@
         spots[l][:, g * SIDE : (g + 1) * SIDE] for g in range(pairs // SIDE) for l in range(lag_local)
     ]
     mirror_picks_ref[...] = pick_rows(jnp.concatenate(ordered, axis=1), mirror_picks_ref.shape[1])
-    cols = jnp.concatenate([cols] * 8, axis=1)
+    target = turned(band, n_row, n_row // 2) * n_lag + turned(inner, n_lag, n_lag // 2)
+    cols = jnp.concatenate([target] * 8, axis=1)
     mirror_hits_ref[...] = jnp.where(cols == iota(mirror_hits_ref.shape, 0), 1.0, 0.0).astype(BF16)
 
 
 def mirror_kernel(
-    n_col, n_lag, lag_local, mats_ref, got_ref, picks_ref, hits_ref, spread_ref, out_ref, sides, turned, held
+    n_row, n_col, n_lag, lag_local, mats_ref, got_ref, picks_ref, hits_ref, spread_ref, out_ref, sides, whole, held
 ):
     pairs = hits_ref.shape[1] // 8
     block = got_ref.shape[1]
@@ -132,9 +146,9 @@
     per_group = SIDE * lag_local
     own = n_lag * lag_local
     chunk = own + n_lag
-    group_past = jnp.concatenate([got_ref[pl.ds(c * chunk, own), :] for c in range(n_col)], axis=0)
+    group_past = jnp.concatenate([got_ref[pl.ds(COL_ORDER.index(c) * chunk, own), :] for c in range(n_col)], axis=0)
     columns = select(picks_ref[...], group_past).T
-    turned[...] = columns
+    whole[...] = columns
     high = columns.astype(BF16).astype(F32)
     low = columns - high
     for g in range(groups):
@@ -153,7 +167,7 @@
                         factor = wide[:, first : first + block]
                     else:
                         lane = jnp.full((block, terms), g * per_group + l * SIDE + q + t, jnp.int32)
-                        factor = jnp.take_along_axis(turned[...], lane, axis=1, mode="promise_in_bounds")
+                        factor = jnp.take_along_axis(whole[...], lane, axis=1, mode="promise_in_bounds")
                     product = mats_ref[p * lag_local + l] * factor
                     acc = acc + jnp.sum(product.reshape(block // 8, 8, block), axis=0)
                 held[pl.ds(p, 8, stride=pairs), :] = acc
@@ -162,14 +176,16 @@
     fields = got_ref[pl.ds(own, n_lag), :]
     for c in range(1, n_col):
         fields = fields + got_ref[pl.ds(c * chunk + own, n_lag), :]
-    mine = pl.ds(pl.multiple_of(lax.axis_index("row") * n_lag, n_lag), n_lag)
+    mine = lax.rem(lax.axis_index("row") + n_row - n_row // 2, n_row) * n_lag
+    mine = pl.ds(pl.multiple_of(mine, n_lag), n_lag)
     out_ref[mine, :] = out_ref[mine, :] + fields
 
 
 def final_kernel(got_ref, incident_ref, inverse_ref, out_ref):
     rhs = incident_ref[...] - jnp.sum(got_ref[...], axis=0, keepdims=True)
     sums = jnp.sum(inverse_ref[...] * rhs, axis=1, keepdims=True)
-    out_ref[...] = jnp.broadcast_to(sums, inverse_ref.shape).T[:1]
+    shape = inverse_ref.shape
+    out_ref[...] = jnp.sum(jnp.where(iota(shape, 0) == iota(shape, 1), sums, 0.0), axis=0, keepdims=True)
 
 
 def call(kernel, name, outs, operands, limit, scratch=()):
@@ -207,7 +223,7 @@
         MIB,
     )
     send, picks, hits = call(
-        functools.partial(order_kernel, n_row),
+        functools.partial(order_kernel, n_lag, n_row),
         "order",
         [((n_row * lags, block), F32), ((terms, n_row * lags), BF16), ((pairs, block), F32)],
         [step_index.reshape(1, 1), history.reshape(lags, block), rows, cols, mask, token],
@@ -217,16 +233,18 @@
         send.reshape(n_src, lag_local, block), ("row", "lag"), 0, 0, tiled=True
     ).reshape(n_row * lags, block)
     sent, mirror_picks, mirror_hits = call(
-        functools.partial(forward_kernel, n_col, n_lag),
+        functools.partial(forward_kernel, n_row, n_col, n_lag),
         "forward",
         [((n_col * chunk, block), F32), ((terms, n_col * own), BF16), ((n_src, 8 * pairs), BF16)],
         [rows, cols, mask, mats, source, picks, hits],
         2 * MIB,
         [((terms, block), F32)],
     )
-    got = lax.all_to_all(sent.reshape(n_col, chunk, block), "col", 0, 0, tiled=True)
+    got = lax.all_to_all(
+        sent.reshape(n_col, chunk, block), "col", 0, 0, tiled=True, axis_index_groups=[list(COL_ORDER)]
+    )
     (mirrored,) = call(
-        functools.partial(mirror_kernel, n_col, n_lag, lag_local),
+        functools.partial(mirror_kernel, n_row, n_col, n_lag, lag_local),
         "mirror",
         [((n_src, block), F32)],
         [mats, got.reshape(n_col * chunk, block), mirror_picks, mirror_hits, spread],
@@ -237,7 +255,12 @@
             ((8 * pairs, block), F32),
         ],
     )
-    fields = lax.all_to_all(mirrored.reshape(n_src, 1, block), ("row", "lag"), 0, 0, tiled=True)
+    last_order = [
+        (r + n_row // 2) % n_row * n_lag + (l + n_lag // 2) % n_lag for r in range(n_row) for l in range(n_lag)
+    ]
+    fields = lax.all_to_all(
+        mirrored.reshape(n_src, 1, block), ("row", "lag"), 0, 0, tiled=True, axis_index_groups=[last_order]
+    )
     return call(
         final_kernel,
         "final",

time: 49.2 us -> 43.8 us (0.89)
  blocking collectives: 44.7 us -> 39.4 us
    all_to_all x1, blocking collectives: 16.6 us -> 13.9 us  [per_device(): lax.all_to_all(sent.reshape(n_col, chunk, block), 'col', 0, 0, tiled=True...]
    all_to_all x1, blocking collectives: 12.2 us -> 9.59 us  [per_device(): lax.all_to_all(mirrored.reshape(n_src, 1, block), ('row', 'lag'), 0, 0, t...]
where the time goes in v5:
time: 43.8 us; the launch traced here: 43.6 us
  blocking collectives  39.4 us (90%)
  Pallas kernels  3.24 us (7%)
  between operations  0.88 us (2%)
    all_to_all x1, blocking collectives, per_device(): lax.all_to_all(send.reshape(n_src, lag_local, block), ('row', 'lag'), 0,...  16 us
    all_to_all x1, blocking collectives, per_device(): lax.all_to_all(sent.reshape(n_col, chunk, block), 'col', 0, 0, tiled=True...  13.9 us
    all_to_all x1, blocking collectives, per_device(): lax.all_to_all(mirrored.reshape(n_src, 1, block), ('row', 'lag'), 0, 0, t...  9.59 us
    pallas_call x5, Pallas kernels, call(): pl.pallas_call(kernel, out_shape=tuple((jax.ShapeDtypeStruct(*out) for ou...  3.24 us

profile of v5, /device:TPU:1, one launch (start us, length us, event | category | flops | bytes accessed | tf_op | source)
XLA Modules:
  0.0 43.6 jit_solution(15635850676156045436)
XLA Ops:
  0.0 0.0 copy-start.2
  0.0 0.0 copy-start.4
  0.0 0.0 copy-start.3
  0.0 0.0 copy-start.1
  0.0 0.0 slice-start
  0.9 0.0 copy-done.2
  0.9 0.0 copy-done.4
  0.9 0.0 copy-done.3
  0.9 0.0 copy-done.1
  0.9 0.0 slice-start.1
  0.9 0.2 order.1
  1.1 16.0 %all_to_all.15 = f32[32,4,128]{2,1,0:T(4,128)S(1)} all-to-all(f32[32,4,128]{2,1,0:T(4,128)S(1)} %bitcast.21), channel_id=1, replica_groups=mesh['row'=4,'col'=8,'lag'=8] {'row','lag'}, dimensions={0} | all-to-all | bytes 131072 | tf_op jit(solution)/shard_map/all_to_all | solution.py:232
  17.1 0.0 slice-done
  17.1 0.0 slice-done.1
  17.1 1.0 %forward.1 = (f32[320,128]{1,0:T(8,128)S(1)}, bf16[128,256]{1,0:T(8,128)(2,1)S(1)}, bf16[32,256]{1,0:T(8,128)(2,1)S(1)}) custom-call(s32[1,32]{1,0:T(1,128)S(1)} %bitcast.33, s32[1,32]{1,0:T(1,128)S(1)} %bitcast.35, s32[4,32]{1,0:T(4,128)S(1)} %bitcast.31, f32[128,128,128]{2,1,0:T(8,128)S(1)} %bitcast.26, f32[128,128]{1,0:T(8,128)S(1)} %bitcast.20, ...), custom_call_target="tpu_custom_call" | custom-call | flops 20000000000 | bytes 67108864 | tf_op jit(solution)/shard_map/forward/pallas_call | solution.py:192
  18.1 13.9 %all_to_all.16 = f32[8,40,128]{2,1,0:T(8,128)S(1)} all-to-all(f32[8,40,128]{2,1,0:T(8,128)S(1)} %bitcast.18), channel_id=1, replica_groups={{40,32,48,24,56,16,0,8},{41,33,49,25,57,17,1,9},{42,34,50,26,58,18,2,10..., dimensions={0} | all-to-all | bytes 327680 | tf_op jit(solution)/shard_map/all_to_all | solution.py:243
  31.9 0.0 copy-start
  31.9 0.0 copy-start.5
  31.9 1.4 %mirror.1 = f32[32,128]{1,0:T(8,128)S(1)} custom-call(f32[128,128,128]{2,1,0:T(8,128)S(1)} %bitcast.27, f32[320,128]{1,0:T(8,128)S(1)} %bitcast.19, bf16[128,256]{1,0:T(8,128)(2,1)S(1)} %get-tuple-element.18.picks_ref, bf16[32,256]{1,0:T(8,128)(2,1)S(1)} %get-tuple-element.19.hits_ref, bf16[4,48,768]{2,1,0:T(8,128)(2,1)S(1)} %get-tuple-element.20.spread_ref), custom_call_target="tpu_custom_call" | custom-call | flops 20000000000 | bytes 67108864 | tf_op jit(solution)/shard_map/mirror/pallas_call | solution.py:192
  33.4 9.6 %all_to_all.17 = f32[32,1,128]{2,1,0:T(1,128)S(1)} all-to-all(f32[32,1,128]{2,1,0:T(1,128)S(1)} %bitcast.22), channel_id=1, replica_groups={{132,133,134,135,128,129,130,131,196,197,198,199,192,193,194,195,4,5,6,..., dimensions={0} | all-to-all | bytes 32768 | tf_op jit(solution)/shard_map/all_to_all | solution.py:261
  43.0 0.0 copy-done
  43.0 0.0 copy-done.5
  43.0 0.6 %final.1 = f32[1,128]{1,0:T(1,128)} custom-call(f32[32,128]{1,0:T(8,128)S(1)} %bitcast.23, f32[1,128]{1,0:T(1,128)S(1)} %copy-done.5, f32[128,128]{1,0:T(8,128)S(1)} %bitcast.28), custom_call_target="tpu_custom_call" | custom-call | flops 20000000000 | bytes 67108864 | tf_op jit(solution)/shard_map/final/pallas_call | solution.py:192
  (2 shorter events, 0.0 us)
Async XLA Ops:
  0.0 0.9 %copy-start.2 = (s32[1,1,32,4]{2,3,1,0:T(4,128)S(1)}, s32[1,1,32,4]{2,3,1,0:T(4,128)}, u32[]{:S(2)}) copy-start(s32[1,1,32,4]{2,3,1,0:T(4,128)} %param.12) | copy-start | bytes 1540
  0.0 0.9 %copy-start.4 = (s32[1,1,32]{2,1,0:T(1,128)S(1)}, s32[1,1,32]{2,1,0:T(1,128)}, u32[]{:S(2)}) copy-start(s32[1,1,32]{2,1,0:T(1,128)} %param.11) | copy-start | bytes 388
  0.0 0.9 %copy-start.3 = (s32[1,1,32]{2,1,0:T(1,128)S(1)}, s32[1,1,32]{2,1,0:T(1,128)}, u32[]{:S(2)}) copy-start(s32[1,1,32]{2,1,0:T(1,128)} %param.10) | copy-start | bytes 388
  0.0 0.9 %copy-start.1 = (f32[32,1,128]{2,1,0:T(1,128)S(1)}, f32[32,1,128]{2,1,0:T(1,128)}, u32[]{:S(2)}) copy-start(f32[32,1,128]{2,1,0:T(1,128)} %param.8) | copy-start | bytes 49156
  0.0 17.1 %slice-start = ((s8[8388608]{0:T(1024)(128)(4,1)}), s8[4194304]{0:T(1024)(128)(4,1)S(1)}, s32[]{:S(2)}) async-start(s8[8388608]{0:T(1024)(128)(4,1)} %bitcast.24), calls=%async_computation.3 | async-start | bytes 8388608
  0.9 16.2 %slice-start.1 = ((s8[8388608]{0:T(1024)(128)(4,1)}), s8[4194304]{0:T(1024)(128)(4,1)S(1)}, s32[]{:S(2)}) async-start(s8[8388608]{0:T(1024)(128)(4,1)} %bitcast.24), calls=%async_computation.4 | async-start | bytes 8388608
  31.9 11.0 %copy-start = (f32[1,128,128]{2,1,0:T(8,128)S(1)}, f32[1,128,128]{2,1,0:T(8,128)}, u32[]{:S(2)}) copy-start(f32[1,128,128]{2,1,0:T(8,128)} %param.15) | copy-start | bytes 196612
  31.9 11.0 %copy-start.5 = (f32[1,128]{1,0:T(1,128)S(1)}, f32[1,128]{1,0:T(1,128)}, u32[]{:S(2)}) copy-start(f32[1,128]{1,0:T(1,128)} %incident_ref.1) | copy-start | bytes 1540

commit v6 on v5

--- a/solution.py
+++ b/solution.py
@@ -15,6 +15,7 @@
 SPREAD = 3
 TOGETHER = 2
 COL_ORDER = (5, 4, 6, 3, 7, 2, 0, 1)
+ROW_FIRST, LAG_FIRST = 2, 5
 
 
 def iota(shape, dim):
@@ -72,12 +73,24 @@
     return major, index - major * size
 
 
+def row_lag_spot(index, n_row, n_lag):
+    major, minor = parts_of(index, n_lag)
+    return turned(major, n_row, ROW_FIRST) * n_lag + turned(minor, n_lag, LAG_FIRST)
+
+
+def col_lag_spot(index, n_lag):
+    major, minor = parts_of(index, n_lag)
+    return major * n_lag + turned(minor, n_lag, LAG_FIRST)
+
+
 def order_kernel(
     n_lag, copies, step_ref, hist_ref, rows_ref, cols_ref, mask_ref, token_ref, send_ref, picks_ref, hits_ref
 ):
     del token_ref
     lags = hist_ref.shape[0]
-    slot = step_ref[...].astype(F32) - 1.0 - iota((lags, lags), 0)
+    lag_local = mask_ref.shape[0]
+    lag = turned(iota((lags, lags), 0), lags, lags - LAG_FIRST * lag_local)
+    slot = step_ref[...].astype(F32) - 1.0 - lag
     slot = jnp.where(slot < 0.0, slot + lags, slot)
     turn = jnp.where(slot == iota((lags, lags), 1), 1.0, 0.0).astype(BF16)
     high, mid, low = (jnp.dot(turn, part, preferred_element_type=F32) for part in split(hist_ref[...], 3))
@@ -85,12 +98,10 @@
     for k in range(copies):
         send_ref[pl.ds(k * lags, lags), :] = past
 
-    lag_local = mask_ref.shape[0]
-    cols = cols_ref[...].astype(F32) * lag_local
+    cols = row_lag_spot(cols_ref[...].astype(F32), copies, n_lag) * lag_local
     spots = [jnp.where(mask_ref[pl.ds(l, 1), :] != 0, cols + l, -1.0) for l in range(lag_local)]
     picks_ref[...] = pick_rows(jnp.concatenate(spots, axis=1), picks_ref.shape[1])
-    major, minor = parts_of(rows_ref[...].astype(F32), n_lag)
-    rows = as_column(major * n_lag + turned(minor, n_lag, n_lag // 2), hits_ref.shape[1])
+    rows = as_column(col_lag_spot(rows_ref[...].astype(F32), n_lag), hits_ref.shape[1])
     hits_ref[...] = jnp.where(rows == iota(hits_ref.shape, 1), 1.0, 0.0)
 
 
@@ -103,7 +114,8 @@
     own = n_lag * lag_local
     chunk = own + n_lag
     vecs[...] = select(picks_ref[...], src_ref[...])
-    group = src_ref[pl.ds(pl.multiple_of(lax.axis_index("row") * own, own), own), :]
+    mine = lax.rem(lax.axis_index("row") + n_row - ROW_FIRST, n_row) * own
+    group = src_ref[pl.ds(pl.multiple_of(mine, own), own), :]
     total = jnp.zeros((block, block), F32)
     for p in range(pairs):
         acc = mats_ref[p * lag_local] * vecs[pl.ds(p, 1), :]
@@ -123,16 +135,16 @@
     band, inner = parts_of(cols, n_lag)
     col_global = band * (n_col * n_lag) + col_base + inner
     off_diag = row_base + rows != col_global
+    places = col_lag_spot(rows, n_lag) * lag_local
     spots = [
-        jnp.where(jnp.logical_and(mask_ref[pl.ds(l, 1), :] != 0, off_diag), rows * lag_local + l, -1.0)
+        jnp.where(jnp.logical_and(mask_ref[pl.ds(l, 1), :] != 0, off_diag), places + l, -1.0)
         for l in range(lag_local)
     ]
     ordered = [
         spots[l][:, g * SIDE : (g + 1) * SIDE] for g in range(pairs // SIDE) for l in range(lag_local)
     ]
     mirror_picks_ref[...] = pick_rows(jnp.concatenate(ordered, axis=1), mirror_picks_ref.shape[1])
-    target = turned(band, n_row, n_row // 2) * n_lag + turned(inner, n_lag, n_lag // 2)
-    cols = jnp.concatenate([target] * 8, axis=1)
+    cols = jnp.concatenate([row_lag_spot(cols, n_row, n_lag)] * 8, axis=1)
     mirror_hits_ref[...] = jnp.where(cols == iota(mirror_hits_ref.shape, 0), 1.0, 0.0).astype(BF16)
 
 
@@ -176,7 +188,7 @@
     fields = got_ref[pl.ds(own, n_lag), :]
     for c in range(1, n_col):
         fields = fields + got_ref[pl.ds(c * chunk + own, n_lag), :]
-    mine = lax.rem(lax.axis_index("row") + n_row - n_row // 2, n_row) * n_lag
+    mine = lax.rem(lax.axis_index("row") + n_row - ROW_FIRST, n_row) * n_lag
     mine = pl.ds(pl.multiple_of(mine, n_lag), n_lag)
     out_ref[mine, :] = out_ref[mine, :] + fields
 
@@ -229,8 +241,11 @@
         [step_index.reshape(1, 1), history.reshape(lags, block), rows, cols, mask, token],
         MIB,
     )
+    row_lag_order = [
+        (r + ROW_FIRST) % n_row * n_lag + (l + LAG_FIRST) % n_lag for r in range(n_row) for l in range(n_lag)
+    ]
     source = lax.all_to_all(
-        send.reshape(n_src, lag_local, block), ("row", "lag"), 0, 0, tiled=True
+        send.reshape(n_src, lag_local, block), ("row", "lag"), 0, 0, tiled=True, axis_index_groups=[row_lag_order]
     ).reshape(n_row * lags, block)
     sent, mirror_picks, mirror_hits = call(
         functools.partial(forward_kernel, n_row, n_col, n_lag),
@@ -255,11 +270,8 @@
             ((8 * pairs, block), F32),
         ],
     )
-    last_order = [
-        (r + n_row // 2) % n_row * n_lag + (l + n_lag // 2) % n_lag for r in range(n_row) for l in range(n_lag)
-    ]
     fields = lax.all_to_all(
-        mirrored.reshape(n_src, 1, block), ("row", "lag"), 0, 0, tiled=True, axis_index_groups=[last_order]
+        mirrored.reshape(n_src, 1, block), ("row", "lag"), 0, 0, tiled=True, axis_index_groups=[row_lag_order]
     )
     return call(
         final_kernel,

time: 43.8 us -> 40.9 us (0.934)
  blocking collectives: 39.4 us -> 36.5 us
    all_to_all x1, blocking collectives: 16 us -> 12.4 us  [per_device(): lax.all_to_all(send.reshape(n_src, lag_local, block), ('row', 'lag'), 0,...]
    all_to_all x1, blocking collectives: 9.59 us -> 10.4 us  [per_device(): lax.all_to_all(mirrored.reshape(n_src, 1, block), ('row', 'lag'), 0, 0, t...]
where the time goes in v6:
time: 40.9 us; the launch traced here: 40.7 us
  blocking collectives  36.5 us (89%)
  Pallas kernels  3.24 us (8%)
  between operations  0.89 us (2%)
    all_to_all x1, blocking collectives, per_device(): lax.all_to_all(sent.reshape(n_col, chunk, block), 'col', 0, 0, tiled=True...  13.8 us
    all_to_all x1, blocking collectives, per_device(): lax.all_to_all(send.reshape(n_src, lag_local, block), ('row', 'lag'), 0,...  12.4 us
    all_to_all x1, blocking collectives, per_device(): lax.all_to_all(mirrored.reshape(n_src, 1, block), ('row', 'lag'), 0, 0, t...  10.4 us
    pallas_call x5, Pallas kernels, call(): pl.pallas_call(kernel, out_shape=tuple((jax.ShapeDtypeStruct(*out) for ou...  3.24 us

profile of v6, /device:TPU:1, one launch (start us, length us, event | category | flops | bytes accessed | tf_op | source)
XLA Modules:
  0.0 40.7 jit_solution(8901403923330287972)
XLA Ops:
  0.0 0.0 copy-start.2
  0.0 0.0 copy-start.4
  0.0 0.0 copy-start.3
  0.0 0.0 copy-start.1
  0.0 0.0 slice-start
  0.9 0.0 copy-done.2
  0.9 0.0 copy-done.4
  0.9 0.0 copy-done.3
  0.9 0.0 copy-done.1
  0.9 0.0 slice-start.1
  0.9 0.2 order.1
  1.1 12.4 %all_to_all.15 = f32[32,4,128]{2,1,0:T(4,128)S(1)} all-to-all(f32[32,4,128]{2,1,0:T(4,128)S(1)} %bitcast.21), channel_id=1, replica_groups={{133,134,135,128,129,130,131,132,197,198,199,192,193,194,195,196,5,6,7,..., dimensions={0} | all-to-all | bytes 131072 | tf_op jit(solution)/shard_map/all_to_all | solution.py:247
  13.5 0.0 slice-done
  13.6 0.0 slice-done.1
  13.6 1.0 %forward.1 = (f32[320,128]{1,0:T(8,128)S(1)}, bf16[128,256]{1,0:T(8,128)(2,1)S(1)}, bf16[32,256]{1,0:T(8,128)(2,1)S(1)}) custom-call(s32[1,32]{1,0:T(1,128)S(1)} %bitcast.33, s32[1,32]{1,0:T(1,128)S(1)} %bitcast.35, s32[4,32]{1,0:T(4,128)S(1)} %bitcast.31, f32[128,128,128]{2,1,0:T(8,128)S(1)} %bitcast.26, f32[128,128]{1,0:T(8,128)S(1)} %bitcast.20, ...), custom_call_target="tpu_custom_call" | custom-call | flops 20000000000 | bytes 67108864 | tf_op jit(solution)/shard_map/forward/pallas_call | solution.py:204
  14.5 13.8 %all_to_all.16 = f32[8,40,128]{2,1,0:T(8,128)S(1)} all-to-all(f32[8,40,128]{2,1,0:T(8,128)S(1)} %bitcast.18), channel_id=1, replica_groups={{40,32,48,24,56,16,0,8},{41,33,49,25,57,17,1,9},{42,34,50,26,58,18,2,10..., dimensions={0} | all-to-all | bytes 327680 | tf_op jit(solution)/shard_map/all_to_all | solution.py:258
  28.3 0.0 copy-start
  28.3 0.0 copy-start.5
  28.3 1.4 %mirror.1 = f32[32,128]{1,0:T(8,128)S(1)} custom-call(f32[128,128,128]{2,1,0:T(8,128)S(1)} %bitcast.27, f32[320,128]{1,0:T(8,128)S(1)} %bitcast.19, bf16[128,256]{1,0:T(8,128)(2,1)S(1)} %get-tuple-element.18.picks_ref, bf16[32,256]{1,0:T(8,128)(2,1)S(1)} %get-tuple-element.19.hits_ref, bf16[4,48,768]{2,1,0:T(8,128)(2,1)S(1)} %get-tuple-element.20.spread_ref), custom_call_target="tpu_custom_call" | custom-call | flops 20000000000 | bytes 67108864 | tf_op jit(solution)/shard_map/mirror/pallas_call | solution.py:204
  29.7 10.4 %all_to_all.17 = f32[32,1,128]{2,1,0:T(1,128)S(1)} all-to-all(f32[32,1,128]{2,1,0:T(1,128)S(1)} %bitcast.22), channel_id=1, replica_groups={{133,134,135,128,129,130,131,132,197,198,199,192,193,194,195,196,5,6,7,..., dimensions={0} | all-to-all | bytes 32768 | tf_op jit(solution)/shard_map/all_to_all | solution.py:273
  40.1 0.0 copy-done
  40.1 0.0 copy-done.5
  40.1 0.6 %final.1 = f32[1,128]{1,0:T(1,128)} custom-call(f32[32,128]{1,0:T(8,128)S(1)} %bitcast.23, f32[1,128]{1,0:T(1,128)S(1)} %copy-done.5, f32[128,128]{1,0:T(8,128)S(1)} %bitcast.28), custom_call_target="tpu_custom_call" | custom-call | flops 20000000000 | bytes 67108864 | tf_op jit(solution)/shard_map/final/pallas_call | solution.py:204
  (2 shorter events, 0.0 us)
Async XLA Ops:
  0.0 0.9 %copy-start.2 = (s32[1,1,32,4]{2,3,1,0:T(4,128)S(1)}, s32[1,1,32,4]{2,3,1,0:T(4,128)}, u32[]{:S(2)}) copy-start(s32[1,1,32,4]{2,3,1,0:T(4,128)} %param.12) | copy-start | bytes 1540
  0.0 0.9 %copy-start.4 = (s32[1,1,32]{2,1,0:T(1,128)S(1)}, s32[1,1,32]{2,1,0:T(1,128)}, u32[]{:S(2)}) copy-start(s32[1,1,32]{2,1,0:T(1,128)} %param.11) | copy-start | bytes 388
  0.0 0.9 %copy-start.3 = (s32[1,1,32]{2,1,0:T(1,128)S(1)}, s32[1,1,32]{2,1,0:T(1,128)}, u32[]{:S(2)}) copy-start(s32[1,1,32]{2,1,0:T(1,128)} %param.10) | copy-start | bytes 388
  0.0 0.9 %copy-start.1 = (f32[32,1,128]{2,1,0:T(1,128)S(1)}, f32[32,1,128]{2,1,0:T(1,128)}, u32[]{:S(2)}) copy-start(f32[32,1,128]{2,1,0:T(1,128)} %param.8) | copy-start | bytes 49156
  0.0 13.5 %slice-start = ((s8[8388608]{0:T(1024)(128)(4,1)}), s8[4194304]{0:T(1024)(128)(4,1)S(1)}, s32[]{:S(2)}) async-start(s8[8388608]{0:T(1024)(128)(4,1)} %bitcast.24), calls=%async_computation.3 | async-start | bytes 8388608
  0.9 12.6 %slice-start.1 = ((s8[8388608]{0:T(1024)(128)(4,1)}), s8[4194304]{0:T(1024)(128)(4,1)S(1)}, s32[]{:S(2)}) async-start(s8[8388608]{0:T(1024)(128)(4,1)} %bitcast.24), calls=%async_computation.4 | async-start | bytes 8388608
  28.3 11.8 %copy-start = (f32[1,128,128]{2,1,0:T(8,128)S(1)}, f32[1,128,128]{2,1,0:T(8,128)}, u32[]{:S(2)}) copy-start(f32[1,128,128]{2,1,0:T(8,128)} %param.15) | copy-start | bytes 196612
  28.3 11.8 %copy-start.5 = (f32[1,128]{1,0:T(1,128)S(1)}, f32[1,128]{1,0:T(1,128)}, u32[]{:S(2)}) copy-start(f32[1,128]{1,0:T(1,128)} %incident_ref.1) | copy-start | bytes 1540

commit v7 on v6

--- a/solution.py
+++ b/solution.py
@@ -149,7 +149,7 @@
 
 
 def mirror_kernel(
-    n_row, n_col, n_lag, lag_local, mats_ref, got_ref, picks_ref, hits_ref, spread_ref, out_ref, sides, whole, held
+    n_row, n_col, n_lag, lag_local, mats_ref, got_ref, picks_ref, hits_ref, spread_ref, out_ref, sides, held
 ):
     pairs = hits_ref.shape[1] // 8
     block = got_ref.shape[1]
@@ -160,7 +160,6 @@
     chunk = own + n_lag
     group_past = jnp.concatenate([got_ref[pl.ds(COL_ORDER.index(c) * chunk, own), :] for c in range(n_col)], axis=0)
     columns = select(picks_ref[...], group_past).T
-    whole[...] = columns
     high = columns.astype(BF16).astype(F32)
     low = columns - high
     for g in range(groups):
@@ -179,7 +178,7 @@
                         factor = wide[:, first : first + block]
                     else:
                         lane = jnp.full((block, terms), g * per_group + l * SIDE + q + t, jnp.int32)
-                        factor = jnp.take_along_axis(whole[...], lane, axis=1, mode="promise_in_bounds")
+                        factor = jnp.take_along_axis(columns, lane, axis=1, mode="promise_in_bounds")
                     product = mats_ref[p * lag_local + l] * factor
                     acc = acc + jnp.sum(product.reshape(block // 8, 8, block), axis=0)
                 held[pl.ds(p, 8, stride=pairs), :] = acc
@@ -200,7 +199,7 @@
     out_ref[...] = jnp.sum(jnp.where(iota(shape, 0) == iota(shape, 1), sums, 0.0), axis=0, keepdims=True)
 
 
-def call(kernel, name, outs, operands, limit, scratch=()):
+def call(kernel, name, outs, operands, limit, scratch=(), flops=20 * 10**9):
     return pl.pallas_call(
         kernel,
         out_shape=tuple(jax.ShapeDtypeStruct(*out) for out in outs),
@@ -209,7 +208,7 @@
         scratch_shapes=[pltpu.VMEM(*item) for item in scratch],
         name=name,
         compiler_params=pltpu.CompilerParams(vmem_limit_bytes=limit),
-        cost_estimate=pl.CostEstimate(flops=20_000_000_000, bytes_accessed=64 * MIB, transcendentals=0),
+        cost_estimate=pl.CostEstimate(flops=flops, bytes_accessed=flops // 300, transcendentals=0),
     )(*operands)
 
 
@@ -233,6 +232,7 @@
         [((SIDE // TOGETHER, 2 * SPREAD * SIDE, TOGETHER * SPREAD * block), BF16), ((8, block), F32)],
         [],
         MIB,
+        flops=20000000000,
     )
     send, picks, hits = call(
         functools.partial(order_kernel, n_lag, n_row),
@@ -240,6 +240,7 @@
         [((n_row * lags, block), F32), ((terms, n_row * lags), BF16), ((pairs, block), F32)],
         [step_index.reshape(1, 1), history.reshape(lags, block), rows, cols, mask, token],
         MIB,
+        flops=200 * 10**9,
     )
     row_lag_order = [
         (r + ROW_FIRST) % n_row * n_lag + (l + LAG_FIRST) % n_lag for r in range(n_row) for l in range(n_lag)
@@ -266,7 +267,6 @@
         3 * MIB,
         [
             ((pairs // SIDE, block, 2 * SPREAD * SIDE), BF16),
-            ((block, terms), F32),
             ((8 * pairs, block), F32),
         ],
     )

time: 40.9 us -> 40.8 us (level)
  no operation moved by 1% of the time
where the time goes in v7:
time: 40.8 us; the launch traced here: 40.6 us
  blocking collectives  36.5 us (89%)
  Pallas kernels  3.24 us (8%)
  between operations  0.72 us (2%)
    all_to_all x1, blocking collectives, per_device(): lax.all_to_all(sent.reshape(n_col, chunk, block), 'col', 0, 0, tiled=True...  13.8 us
    all_to_all x1, blocking collectives, per_device(): lax.all_to_all(send.reshape(n_src, lag_local, block), ('row', 'lag'), 0,...  12.4 us
    all_to_all x1, blocking collectives, per_device(): lax.all_to_all(mirrored.reshape(n_src, 1, block), ('row', 'lag'), 0, 0, t...  10.3 us
    pallas_call x5, Pallas kernels, call(): pl.pallas_call(kernel, out_shape=tuple((jax.ShapeDtypeStruct(*out) for ou...  3.24 us

profile of v7, /device:TPU:1, one launch (start us, length us, event | category | flops | bytes accessed | tf_op | source)
XLA Modules:
  0.0 40.6 jit_solution(5142497313897249746)
XLA Ops:
  0.0 0.0 copy-start.3
  0.0 0.0 copy-start.5
  0.0 0.0 copy-start.4
  0.0 0.0 copy-start.2
  0.7 0.0 copy-done.3
  0.7 0.0 copy-done.5
  0.7 0.0 copy-done.4
  0.7 0.0 copy-done.2
  0.8 0.0 copy-start
  0.8 0.2 order.1
  1.0 12.4 %all_to_all.15 = f32[32,4,128]{2,1,0:T(4,128)S(1)} all-to-all(f32[32,4,128]{2,1,0:T(4,128)S(1)} %bitcast.21), channel_id=1, replica_groups={{133,134,135,128,129,130,131,132,197,198,199,192,193,194,195,196,5,6,7,..., dimensions={0} | all-to-all | bytes 131072 | tf_op jit(solution)/shard_map/all_to_all | solution.py:248
  13.4 0.0 copy-done
  13.4 1.0 %forward.1 = (f32[320,128]{1,0:T(8,128)S(1)}, bf16[128,256]{1,0:T(8,128)(2,1)S(1)}, bf16[32,256]{1,0:T(8,128)(2,1)S(1)}) custom-call(s32[1,32]{1,0:T(1,128)S(1)} %bitcast.31, s32[1,32]{1,0:T(1,128)S(1)} %bitcast.33, s32[4,32]{1,0:T(4,128)S(1)} %bitcast.29, f32[128,128,128]{2,1,0:T(8,128)S(1)} %bitcast.24, f32[128,128]{1,0:T(8,128)S(1)} %bitcast.20, ...), custom_call_target="tpu_custom_call" | custom-call | flops 20000000000 | bytes 66666664 | tf_op jit(solution)/shard_map/forward/pallas_call | solution.py:203
  14.4 13.8 %all_to_all.16 = f32[8,40,128]{2,1,0:T(8,128)S(1)} all-to-all(f32[8,40,128]{2,1,0:T(8,128)S(1)} %bitcast.18), channel_id=1, replica_groups={{40,32,48,24,56,16,0,8},{41,33,49,25,57,17,1,9},{42,34,50,26,58,18,2,10..., dimensions={0} | all-to-all | bytes 327680 | tf_op jit(solution)/shard_map/all_to_all | solution.py:259
  28.1 0.0 copy-start.1
  28.1 0.0 copy-start.6
  28.1 1.4 %mirror.1 = f32[32,128]{1,0:T(8,128)S(1)} custom-call(f32[128,128,128]{2,1,0:T(8,128)S(1)} %bitcast.25, f32[320,128]{1,0:T(8,128)S(1)} %bitcast.19, bf16[128,256]{1,0:T(8,128)(2,1)S(1)} %get-tuple-element.18.picks_ref, bf16[32,256]{1,0:T(8,128)(2,1)S(1)} %get-tuple-element.19.hits_ref, bf16[4,48,768]{2,1,0:T(8,128)(2,1)S(1)} %get-tuple-element.20.spread_ref), custom_call_target="tpu_custom_call" | custom-call | flops 20000000000 | bytes 66666664 | tf_op jit(solution)/shard_map/mirror/pallas_call | solution.py:203
  29.6 10.3 %all_to_all.17 = f32[32,1,128]{2,1,0:T(1,128)S(1)} all-to-all(f32[32,1,128]{2,1,0:T(1,128)S(1)} %bitcast.22), channel_id=1, replica_groups={{133,134,135,128,129,130,131,132,197,198,199,192,193,194,195,196,5,6,7,..., dimensions={0} | all-to-all | bytes 32768 | tf_op jit(solution)/shard_map/all_to_all | solution.py:273
  39.9 0.0 copy-done.1
  39.9 0.0 copy-done.6
  39.9 0.6 %final.1 = f32[1,128]{1,0:T(1,128)} custom-call(f32[32,128]{1,0:T(8,128)S(1)} %bitcast.23, f32[1,128]{1,0:T(1,128)S(1)} %copy-done.6, f32[128,128]{1,0:T(8,128)S(1)} %bitcast.26), custom_call_target="tpu_custom_call" | custom-call | flops 20000000000 | bytes 66666664 | tf_op jit(solution)/shard_map/final/pallas_call | solution.py:203
  (1 shorter events, 0.0 us)
Async XLA Ops:
  0.0 0.7 %copy-start.3 = (s32[1,1,32,4]{2,3,1,0:T(4,128)S(1)}, s32[1,1,32,4]{2,3,1,0:T(4,128)}, u32[]{:S(2)}) copy-start(s32[1,1,32,4]{2,3,1,0:T(4,128)} %param.12) | copy-start | bytes 1540
  0.0 0.7 %copy-start.5 = (s32[1,1,32]{2,1,0:T(1,128)S(1)}, s32[1,1,32]{2,1,0:T(1,128)}, u32[]{:S(2)}) copy-start(s32[1,1,32]{2,1,0:T(1,128)} %param.11) | copy-start | bytes 388
  0.0 0.7 %copy-start.4 = (s32[1,1,32]{2,1,0:T(1,128)S(1)}, s32[1,1,32]{2,1,0:T(1,128)}, u32[]{:S(2)}) copy-start(s32[1,1,32]{2,1,0:T(1,128)} %param.10) | copy-start | bytes 388
  0.0 0.8 %copy-start.2 = (f32[32,1,128]{2,1,0:T(1,128)S(1)}, f32[32,1,128]{2,1,0:T(1,128)}, u32[]{:S(2)}) copy-start(f32[32,1,128]{2,1,0:T(1,128)} %param.8) | copy-start | bytes 49156
  0.8 12.6 %copy-start = (f32[1,1,32,4,128,128]{5,4,3,2,1,0:T(8,128)S(1)}, f32[1,1,32,4,128,128]{5,4,3,2,1,0:T(8,128)}, u32[]{:S(2)}) copy-start(f32[1,1,32,4,128,128]{5,4,3,2,1,0:T(8,128)} %param.13) | copy-start | bytes 25165828
  28.1 11.8 %copy-start.1 = (f32[1,128,128]{2,1,0:T(8,128)S(1)}, f32[1,128,128]{2,1,0:T(8,128)}, u32[]{:S(2)}) copy-start(f32[1,128,128]{2,1,0:T(8,128)} %param.15) | copy-start | bytes 196612
  28.1 11.8 %copy-start.6 = (f32[1,128]{1,0:T(1,128)S(1)}, f32[1,128]{1,0:T(1,128)}, u32[]{:S(2)}) copy-start(f32[1,128]{1,0:T(1,128)} %incident_ref.1) | copy-start | bytes 1540

commit v8 on v7

--- a/solution.py
+++ b/solution.py
@@ -11,9 +11,11 @@
 F32 = jnp.float32
 BF16 = jnp.bfloat16
 MIB = 1024 * 1024
+PARTS = 3
 SIDE = 8
 SPREAD = 3
 TOGETHER = 2
+DEPTH = 80
 COL_ORDER = (5, 4, 6, 3, 7, 2, 0, 1)
 ROW_FIRST, LAG_FIRST = 2, 5
 
@@ -22,9 +24,9 @@
     return lax.broadcasted_iota(jnp.int32, shape, dim).astype(F32)
 
 
-def split(values, parts):
+def split(values):
     pieces = []
-    for _ in range(parts - 1):
+    for _ in range(PARTS - 1):
         pieces.append(values.astype(BF16))
         values = values - pieces[-1].astype(F32)
     return pieces + [values.astype(BF16)]
@@ -32,7 +34,7 @@
 
 def select(picks, values):
     return jnp.dot(
-        jnp.concatenate([picks] * 2, axis=1), jnp.concatenate(split(values, 2), axis=0), preferred_element_type=F32
+        jnp.concatenate([picks] * PARTS, axis=1), jnp.concatenate(split(values), axis=0), preferred_element_type=F32
     )
 
 
@@ -58,7 +60,9 @@
                 first = (t * SPREAD + l) * 128
                 lanes = jnp.logical_and(target >= first, target < first + 128)
                 row = l * SIDE + batch * TOGETHER + t
-                rows = jnp.logical_or(source == row, source == row + SPREAD * SIDE)
+                rows = source == row
+                for part in range(1, PARTS):
+                    rows = jnp.logical_or(rows, source == row + part * SPREAD * SIDE)
                 table = jnp.where(jnp.logical_and(lanes, rows), 1.0, table)
         spread_ref[batch] = table.astype(BF16)
 
@@ -93,7 +97,7 @@
     slot = step_ref[...].astype(F32) - 1.0 - lag
     slot = jnp.where(slot < 0.0, slot + lags, slot)
     turn = jnp.where(slot == iota((lags, lags), 1), 1.0, 0.0).astype(BF16)
-    high, mid, low = (jnp.dot(turn, part, preferred_element_type=F32) for part in split(hist_ref[...], 3))
+    high, mid, low = (jnp.dot(turn, part, preferred_element_type=F32) for part in split(hist_ref[...]))
     past = high + (mid + low)
     for k in range(copies):
         send_ref[pl.ds(k * lags, lags), :] = past
@@ -160,11 +164,11 @@
     chunk = own + n_lag
     group_past = jnp.concatenate([got_ref[pl.ds(COL_ORDER.index(c) * chunk, own), :] for c in range(n_col)], axis=0)
     columns = select(picks_ref[...], group_past).T
-    high = columns.astype(BF16).astype(F32)
-    low = columns - high
+    pieces = [piece.astype(F32) for piece in split(columns)]
+    empty = jnp.zeros((block, DEPTH - PARTS * SPREAD * SIDE), F32)
     for g in range(groups):
         keep = slice(g * per_group, g * per_group + SPREAD * SIDE)
-        sides[g] = jnp.concatenate([high[:, keep], low[:, keep]], axis=1).astype(BF16)
+        sides[g] = jnp.concatenate([piece[:, keep] for piece in pieces] + [empty], axis=1).astype(BF16)
     for g in range(groups):
         side = sides[g]
         for q in range(0, SIDE, TOGETHER):
@@ -229,7 +233,7 @@
     spread, token = call(
         table_kernel,
         "table",
-        [((SIDE // TOGETHER, 2 * SPREAD * SIDE, TOGETHER * SPREAD * block), BF16), ((8, block), F32)],
+        [((SIDE // TOGETHER, DEPTH, TOGETHER * SPREAD * block), BF16), ((8, block), F32)],
         [],
         MIB,
         flops=20000000000,
@@ -266,7 +270,7 @@
         [mats, got.reshape(n_col * chunk, block), mirror_picks, mirror_hits, spread],
         3 * MIB,
         [
-            ((pairs // SIDE, block, 2 * SPREAD * SIDE), BF16),
+            ((pairs // SIDE, block, DEPTH), BF16),
             ((8 * pairs, block), F32),
         ],
     )

time: 40.8 us -> 40.9 us (level)
  no operation moved by 1% of the time
where the time goes in v8:
time: 40.9 us; the launch traced here: 40.7 us
  blocking collectives  36.5 us (89%)
  Pallas kernels  3.37 us (8%)
  between operations  0.71 us (2%)
    all_to_all x1, blocking collectives, per_device(): lax.all_to_all(sent.reshape(n_col, chunk, block), 'col', 0, 0, tiled=True...  13.8 us
    all_to_all x1, blocking collectives, per_device(): lax.all_to_all(send.reshape(n_src, lag_local, block), ('row', 'lag'), 0,...  12.4 us
    all_to_all x1, blocking collectives, per_device(): lax.all_to_all(mirrored.reshape(n_src, 1, block), ('row', 'lag'), 0, 0, t...  10.3 us
    pallas_call x5, Pallas kernels, call(): pl.pallas_call(kernel, out_shape=tuple((jax.ShapeDtypeStruct(*out) for ou...  3.37 us

profile of v8, /device:TPU:1, one launch (start us, length us, event | category | flops | bytes accessed | tf_op | source)
XLA Modules:
  0.0 40.7 jit_solution(16486328708313567093)
XLA Ops:
  0.0 0.0 copy-start.3
  0.0 0.0 copy-start.5
  0.0 0.0 copy-start.4
  0.0 0.0 copy-start.2
  0.7 0.0 copy-done.3
  0.7 0.0 copy-done.5
  0.7 0.0 copy-done.4
  0.7 0.0 copy-done.2
  0.8 0.0 copy-start
  0.8 0.2 order.1
  1.0 12.4 %all_to_all.15 = f32[32,4,128]{2,1,0:T(4,128)S(1)} all-to-all(f32[32,4,128]{2,1,0:T(4,128)S(1)} %bitcast.21), channel_id=1, replica_groups={{133,134,135,128,129,130,131,132,197,198,199,192,193,194,195,196,5,6,7,..., dimensions={0} | all-to-all | bytes 131072 | tf_op jit(solution)/shard_map/all_to_all | solution.py:252
  13.4 0.0 copy-done
  13.4 1.0 %forward.1 = (f32[320,128]{1,0:T(8,128)S(1)}, bf16[128,256]{1,0:T(8,128)(2,1)S(1)}, bf16[32,256]{1,0:T(8,128)(2,1)S(1)}) custom-call(s32[1,32]{1,0:T(1,128)S(1)} %bitcast.31, s32[1,32]{1,0:T(1,128)S(1)} %bitcast.33, s32[4,32]{1,0:T(4,128)S(1)} %bitcast.29, f32[128,128,128]{2,1,0:T(8,128)S(1)} %bitcast.24, f32[128,128]{1,0:T(8,128)S(1)} %bitcast.20, ...), custom_call_target="tpu_custom_call" | custom-call | flops 20000000000 | bytes 66666664 | tf_op jit(solution)/shard_map/forward/pallas_call | solution.py:207
  14.4 13.8 %all_to_all.16 = f32[8,40,128]{2,1,0:T(8,128)S(1)} all-to-all(f32[8,40,128]{2,1,0:T(8,128)S(1)} %bitcast.18), channel_id=1, replica_groups={{40,32,48,24,56,16,0,8},{41,33,49,25,57,17,1,9},{42,34,50,26,58,18,2,10..., dimensions={0} | all-to-all | bytes 327680 | tf_op jit(solution)/shard_map/all_to_all | solution.py:263
  28.2 0.0 copy-start.1
  28.2 0.0 copy-start.6
  28.2 1.5 %mirror.1 = f32[32,128]{1,0:T(8,128)S(1)} custom-call(f32[128,128,128]{2,1,0:T(8,128)S(1)} %bitcast.25, f32[320,128]{1,0:T(8,128)S(1)} %bitcast.19, bf16[128,256]{1,0:T(8,128)(2,1)S(1)} %get-tuple-element.18.picks_ref, bf16[32,256]{1,0:T(8,128)(2,1)S(1)} %get-tuple-element.19.hits_ref, bf16[4,80,768]{2,1,0:T(8,128)(2,1)S(1)} %get-tuple-element.20.spread_ref), custom_call_target="tpu_custom_call" | custom-call | flops 20000000000 | bytes 66666664 | tf_op jit(solution)/shard_map/mirror/pallas_call | solution.py:207
  29.7 10.3 %all_to_all.17 = f32[32,1,128]{2,1,0:T(1,128)S(1)} all-to-all(f32[32,1,128]{2,1,0:T(1,128)S(1)} %bitcast.22), channel_id=1, replica_groups={{133,134,135,128,129,130,131,132,197,198,199,192,193,194,195,196,5,6,7,..., dimensions={0} | all-to-all | bytes 32768 | tf_op jit(solution)/shard_map/all_to_all | solution.py:277
  40.0 0.0 copy-done.1
  40.0 0.0 copy-done.6
  40.0 0.6 %final.1 = f32[1,128]{1,0:T(1,128)} custom-call(f32[32,128]{1,0:T(8,128)S(1)} %bitcast.23, f32[1,128]{1,0:T(1,128)S(1)} %copy-done.6, f32[128,128]{1,0:T(8,128)S(1)} %bitcast.26), custom_call_target="tpu_custom_call" | custom-call | flops 20000000000 | bytes 66666664 | tf_op jit(solution)/shard_map/final/pallas_call | solution.py:207
  (1 shorter events, 0.0 us)
Async XLA Ops:
  0.0 0.7 %copy-start.3 = (s32[1,1,32,4]{2,3,1,0:T(4,128)S(1)}, s32[1,1,32,4]{2,3,1,0:T(4,128)}, u32[]{:S(2)}) copy-start(s32[1,1,32,4]{2,3,1,0:T(4,128)} %param.12) | copy-start | bytes 1540
  0.0 0.7 %copy-start.5 = (s32[1,1,32]{2,1,0:T(1,128)S(1)}, s32[1,1,32]{2,1,0:T(1,128)}, u32[]{:S(2)}) copy-start(s32[1,1,32]{2,1,0:T(1,128)} %param.11) | copy-start | bytes 388
  0.0 0.7 %copy-start.4 = (s32[1,1,32]{2,1,0:T(1,128)S(1)}, s32[1,1,32]{2,1,0:T(1,128)}, u32[]{:S(2)}) copy-start(s32[1,1,32]{2,1,0:T(1,128)} %param.10) | copy-start | bytes 388
  0.0 0.8 %copy-start.2 = (f32[32,1,128]{2,1,0:T(1,128)S(1)}, f32[32,1,128]{2,1,0:T(1,128)}, u32[]{:S(2)}) copy-start(f32[32,1,128]{2,1,0:T(1,128)} %param.8) | copy-start | bytes 49156
  0.8 12.6 %copy-start = (f32[1,1,32,4,128,128]{5,4,3,2,1,0:T(8,128)S(1)}, f32[1,1,32,4,128,128]{5,4,3,2,1,0:T(8,128)}, u32[]{:S(2)}) copy-start(f32[1,1,32,4,128,128]{5,4,3,2,1,0:T(8,128)} %param.13) | copy-start | bytes 25165828
  28.2 11.8 %copy-start.1 = (f32[1,128,128]{2,1,0:T(8,128)S(1)}, f32[1,128,128]{2,1,0:T(8,128)}, u32[]{:S(2)}) copy-start(f32[1,128,128]{2,1,0:T(8,128)} %param.15) | copy-start | bytes 196612
  28.2 11.8 %copy-start.6 = (f32[1,128]{1,0:T(1,128)S(1)}, f32[1,128]{1,0:T(1,128)}, u32[]{:S(2)}) copy-start(f32[1,128]{1,0:T(1,128)} %incident_ref.1) | copy-start | bytes 1540

commit v9 on v8

--- a/solution.py
+++ b/solution.py
@@ -148,14 +148,14 @@
         spots[l][:, g * SIDE : (g + 1) * SIDE] for g in range(pairs // SIDE) for l in range(lag_local)
     ]
     mirror_picks_ref[...] = pick_rows(jnp.concatenate(ordered, axis=1), mirror_picks_ref.shape[1])
-    cols = jnp.concatenate([row_lag_spot(cols, n_row, n_lag)] * 8, axis=1)
+    cols = row_lag_spot(cols, n_row, n_lag)
     mirror_hits_ref[...] = jnp.where(cols == iota(mirror_hits_ref.shape, 0), 1.0, 0.0).astype(BF16)
 
 
 def mirror_kernel(
     n_row, n_col, n_lag, lag_local, mats_ref, got_ref, picks_ref, hits_ref, spread_ref, out_ref, sides, held
 ):
-    pairs = hits_ref.shape[1] // 8
+    pairs = hits_ref.shape[1]
     block = got_ref.shape[1]
     terms = lag_local * pairs
     groups = pairs // SIDE
@@ -187,7 +187,7 @@
                     acc = acc + jnp.sum(product.reshape(block // 8, 8, block), axis=0)
                 held[pl.ds(p, 8, stride=pairs), :] = acc
 
-    out_ref[...] = select(hits_ref[...], held[...])
+    out_ref[...] = select(hits_ref[...], jnp.sum(held[...].reshape(8, pairs, block), axis=0))
     fields = got_ref[pl.ds(own, n_lag), :]
     for c in range(1, n_col):
         fields = fields + got_ref[pl.ds(c * chunk + own, n_lag), :]
@@ -255,7 +255,7 @@
     sent, mirror_picks, mirror_hits = call(
         functools.partial(forward_kernel, n_row, n_col, n_lag),
         "forward",
-        [((n_col * chunk, block), F32), ((terms, n_col * own), BF16), ((n_src, 8 * pairs), BF16)],
+        [((n_col * chunk, block), F32), ((terms, n_col * own), BF16), ((n_src, pairs), BF16)],
         [rows, cols, mask, mats, source, picks, hits],
         2 * MIB,
         [((terms, block), F32)],

time: 40.9 us -> 41.1 us (level)
  no operation moved by 1% of the time
where the time goes in v9:
time: 41.1 us; the launch traced here: 40.9 us
  blocking collectives  36.5 us (89%)
  Pallas kernels  3.64 us (9%)
  between operations  0.71 us (2%)
    all_to_all x1, blocking collectives, per_device(): lax.all_to_all(sent.reshape(n_col, chunk, block), 'col', 0, 0, tiled=True...  13.8 us
    all_to_all x1, blocking collectives, per_device(): lax.all_to_all(send.reshape(n_src, lag_local, block), ('row', 'lag'), 0,...  12.4 us
    all_to_all x1, blocking collectives, per_device(): lax.all_to_all(mirrored.reshape(n_src, 1, block), ('row', 'lag'), 0, 0, t...  10.3 us
    pallas_call x5, Pallas kernels, call(): pl.pallas_call(kernel, out_shape=tuple((jax.ShapeDtypeStruct(*out) for ou...  3.64 us

profile of v9, /device:TPU:1, one launch (start us, length us, event | category | flops | bytes accessed | tf_op | source)
XLA Modules:
  0.0 40.9 jit_solution(4147719297932455775)
XLA Ops:
  0.0 0.0 copy-start.3
  0.0 0.0 copy-start.5
  0.0 0.0 copy-start.4
  0.0 0.0 copy-start.2
  0.7 0.0 copy-done.3
  0.7 0.0 copy-done.5
  0.7 0.0 copy-done.4
  0.7 0.0 copy-done.2
  0.8 0.0 copy-start
  0.8 0.2 order.1
  1.0 12.4 %all_to_all.15 = f32[32,4,128]{2,1,0:T(4,128)S(1)} all-to-all(f32[32,4,128]{2,1,0:T(4,128)S(1)} %bitcast.21), channel_id=1, replica_groups={{133,134,135,128,129,130,131,132,197,198,199,192,193,194,195,196,5,6,7,..., dimensions={0} | all-to-all | bytes 131072 | tf_op jit(solution)/shard_map/all_to_all | solution.py:252
  13.4 0.0 copy-done
  13.4 1.1 %forward.1 = (f32[320,128]{1,0:T(8,128)S(1)}, bf16[128,256]{1,0:T(8,128)(2,1)S(1)}, bf16[32,32]{1,0:T(8,128)(2,1)S(1)}) custom-call(s32[1,32]{1,0:T(1,128)S(1)} %bitcast.31, s32[1,32]{1,0:T(1,128)S(1)} %bitcast.33, s32[4,32]{1,0:T(4,128)S(1)} %bitcast.29, f32[128,128,128]{2,1,0:T(8,128)S(1)} %bitcast.24, f32[128,128]{1,0:T(8,128)S(1)} %bitcast.20, ...), custom_call_target="tpu_custom_call" | custom-call | flops 20000000000 | bytes 66666664 | tf_op jit(solution)/shard_map/forward/pallas_call | solution.py:207
  14.5 13.8 %all_to_all.16 = f32[8,40,128]{2,1,0:T(8,128)S(1)} all-to-all(f32[8,40,128]{2,1,0:T(8,128)S(1)} %bitcast.18), channel_id=1, replica_groups={{40,32,48,24,56,16,0,8},{41,33,49,25,57,17,1,9},{42,34,50,26,58,18,2,10..., dimensions={0} | all-to-all | bytes 327680 | tf_op jit(solution)/shard_map/all_to_all | solution.py:263
  28.3 0.0 copy-start.1
  28.3 0.0 copy-start.6
  28.3 1.7 %mirror.1 = f32[32,128]{1,0:T(8,128)S(1)} custom-call(f32[128,128,128]{2,1,0:T(8,128)S(1)} %bitcast.25, f32[320,128]{1,0:T(8,128)S(1)} %bitcast.19, bf16[128,256]{1,0:T(8,128)(2,1)S(1)} %get-tuple-element.18.picks_ref, bf16[32,32]{1,0:T(8,128)(2,1)S(1)} %get-tuple-element.19.hits_ref, bf16[4,80,768]{2,1,0:T(8,128)(2,1)S(1)} %get-tuple-element.20.spread_ref), custom_call_target="tpu_custom_call" | custom-call | flops 20000000000 | bytes 66666664 | tf_op jit(solution)/shard_map/mirror/pallas_call | solution.py:207
  30.0 10.3 %all_to_all.17 = f32[32,1,128]{2,1,0:T(1,128)S(1)} all-to-all(f32[32,1,128]{2,1,0:T(1,128)S(1)} %bitcast.22), channel_id=1, replica_groups={{133,134,135,128,129,130,131,132,197,198,199,192,193,194,195,196,5,6,7,..., dimensions={0} | all-to-all | bytes 32768 | tf_op jit(solution)/shard_map/all_to_all | solution.py:277
  40.3 0.0 copy-done.1
  40.3 0.0 copy-done.6
  40.3 0.6 %final.1 = f32[1,128]{1,0:T(1,128)} custom-call(f32[32,128]{1,0:T(8,128)S(1)} %bitcast.23, f32[1,128]{1,0:T(1,128)S(1)} %copy-done.6, f32[128,128]{1,0:T(8,128)S(1)} %bitcast.26), custom_call_target="tpu_custom_call" | custom-call | flops 20000000000 | bytes 66666664 | tf_op jit(solution)/shard_map/final/pallas_call | solution.py:207
  (1 shorter events, 0.0 us)
Async XLA Ops:
  0.0 0.7 %copy-start.3 = (s32[1,1,32,4]{2,3,1,0:T(4,128)S(1)}, s32[1,1,32,4]{2,3,1,0:T(4,128)}, u32[]{:S(2)}) copy-start(s32[1,1,32,4]{2,3,1,0:T(4,128)} %param.12) | copy-start | bytes 1540
  0.0 0.7 %copy-start.5 = (s32[1,1,32]{2,1,0:T(1,128)S(1)}, s32[1,1,32]{2,1,0:T(1,128)}, u32[]{:S(2)}) copy-start(s32[1,1,32]{2,1,0:T(1,128)} %param.11) | copy-start | bytes 388
  0.0 0.7 %copy-start.4 = (s32[1,1,32]{2,1,0:T(1,128)S(1)}, s32[1,1,32]{2,1,0:T(1,128)}, u32[]{:S(2)}) copy-start(s32[1,1,32]{2,1,0:T(1,128)} %param.10) | copy-start | bytes 388
  0.0 0.8 %copy-start.2 = (f32[32,1,128]{2,1,0:T(1,128)S(1)}, f32[32,1,128]{2,1,0:T(1,128)}, u32[]{:S(2)}) copy-start(f32[32,1,128]{2,1,0:T(1,128)} %param.8) | copy-start | bytes 49156
  0.8 12.6 %copy-start = (f32[1,1,32,4,128,128]{5,4,3,2,1,0:T(8,128)S(1)}, f32[1,1,32,4,128,128]{5,4,3,2,1,0:T(8,128)}, u32[]{:S(2)}) copy-start(f32[1,1,32,4,128,128]{5,4,3,2,1,0:T(8,128)} %param.13) | copy-start | bytes 25165828
  28.3 12.0 %copy-start.1 = (f32[1,128,128]{2,1,0:T(8,128)S(1)}, f32[1,128,128]{2,1,0:T(8,128)}, u32[]{:S(2)}) copy-start(f32[1,128,128]{2,1,0:T(8,128)} %param.15) | copy-start | bytes 196612
  28.3 12.0 %copy-start.6 = (f32[1,128]{1,0:T(1,128)S(1)}, f32[1,128]{1,0:T(1,128)}, u32[]{:S(2)}) copy-start(f32[1,128]{1,0:T(1,128)} %incident_ref.1) | copy-start | bytes 1540

commit v10 on v8

--- a/solution.py
+++ b/solution.py
@@ -14,7 +14,7 @@
 PARTS = 3
 SIDE = 8
 SPREAD = 3
-TOGETHER = 2
+TOGETHER = 4
 DEPTH = 80
 COL_ORDER = (5, 4, 6, 3, 7, 2, 0, 1)
 ROW_FIRST, LAG_FIRST = 2, 5

time: 40.9 us -> 40.9 us (level)
  no operation moved by 1% of the time
where the time goes in v10:
time: 40.9 us; the launch traced here: 40.7 us
  blocking collectives  36.5 us (89%)
  Pallas kernels  3.37 us (8%)
  between operations  0.71 us (2%)
    all_to_all x1, blocking collectives, per_device(): lax.all_to_all(sent.reshape(n_col, chunk, block), 'col', 0, 0, tiled=True...  13.8 us
    all_to_all x1, blocking collectives, per_device(): lax.all_to_all(send.reshape(n_src, lag_local, block), ('row', 'lag'), 0,...  12.4 us
    all_to_all x1, blocking collectives, per_device(): lax.all_to_all(mirrored.reshape(n_src, 1, block), ('row', 'lag'), 0, 0, t...  10.3 us
    pallas_call x5, Pallas kernels, call(): pl.pallas_call(kernel, out_shape=tuple((jax.ShapeDtypeStruct(*out) for ou...  3.37 us

profile of v10, /device:TPU:1, one launch (start us, length us, event | category | flops | bytes accessed | tf_op | source)
XLA Modules:
  0.0 40.7 jit_solution(4858261100445077149)
XLA Ops:
  0.0 0.0 copy-start.3
  0.0 0.0 copy-start.5
  0.0 0.0 copy-start.4
  0.0 0.0 copy-start.2
  0.7 0.0 copy-done.3
  0.7 0.0 copy-done.5
  0.7 0.0 copy-done.4
  0.8 0.0 copy-done.2
  0.8 0.0 copy-start
  0.8 0.2 order.1
  1.0 12.4 %all_to_all.15 = f32[32,4,128]{2,1,0:T(4,128)S(1)} all-to-all(f32[32,4,128]{2,1,0:T(4,128)S(1)} %bitcast.21), channel_id=1, replica_groups={{133,134,135,128,129,130,131,132,197,198,199,192,193,194,195,196,5,6,7,..., dimensions={0} | all-to-all | bytes 131072 | tf_op jit(solution)/shard_map/all_to_all | solution.py:252
  13.4 0.0 copy-done
  13.4 1.0 %forward.1 = (f32[320,128]{1,0:T(8,128)S(1)}, bf16[128,256]{1,0:T(8,128)(2,1)S(1)}, bf16[32,256]{1,0:T(8,128)(2,1)S(1)}) custom-call(s32[1,32]{1,0:T(1,128)S(1)} %bitcast.31, s32[1,32]{1,0:T(1,128)S(1)} %bitcast.33, s32[4,32]{1,0:T(4,128)S(1)} %bitcast.29, f32[128,128,128]{2,1,0:T(8,128)S(1)} %bitcast.24, f32[128,128]{1,0:T(8,128)S(1)} %bitcast.20, ...), custom_call_target="tpu_custom_call" | custom-call | flops 20000000000 | bytes 66666664 | tf_op jit(solution)/shard_map/forward/pallas_call | solution.py:207
  14.4 13.8 %all_to_all.16 = f32[8,40,128]{2,1,0:T(8,128)S(1)} all-to-all(f32[8,40,128]{2,1,0:T(8,128)S(1)} %bitcast.18), channel_id=1, replica_groups={{40,32,48,24,56,16,0,8},{41,33,49,25,57,17,1,9},{42,34,50,26,58,18,2,10..., dimensions={0} | all-to-all | bytes 327680 | tf_op jit(solution)/shard_map/all_to_all | solution.py:263
  28.2 0.0 copy-start.1
  28.2 0.0 copy-start.6
  28.2 1.5 %mirror.1 = f32[32,128]{1,0:T(8,128)S(1)} custom-call(f32[128,128,128]{2,1,0:T(8,128)S(1)} %bitcast.25, f32[320,128]{1,0:T(8,128)S(1)} %bitcast.19, bf16[128,256]{1,0:T(8,128)(2,1)S(1)} %get-tuple-element.18.picks_ref, bf16[32,256]{1,0:T(8,128)(2,1)S(1)} %get-tuple-element.19.hits_ref, bf16[2,80,1536]{2,1,0:T(8,128)(2,1)S(1)} %get-tuple-element.20.spread_ref), custom_call_target="tpu_custom_call" | custom-call | flops 20000000000 | bytes 66666664 | tf_op jit(solution)/shard_map/mirror/pallas_call | solution.py:207
  29.7 10.3 %all_to_all.17 = f32[32,1,128]{2,1,0:T(1,128)S(1)} all-to-all(f32[32,1,128]{2,1,0:T(1,128)S(1)} %bitcast.22), channel_id=1, replica_groups={{133,134,135,128,129,130,131,132,197,198,199,192,193,194,195,196,5,6,7,..., dimensions={0} | all-to-all | bytes 32768 | tf_op jit(solution)/shard_map/all_to_all | solution.py:277
  40.0 0.0 copy-done.1
  40.0 0.0 copy-done.6
  40.0 0.6 %final.1 = f32[1,128]{1,0:T(1,128)} custom-call(f32[32,128]{1,0:T(8,128)S(1)} %bitcast.23, f32[1,128]{1,0:T(1,128)S(1)} %copy-done.6, f32[128,128]{1,0:T(8,128)S(1)} %bitcast.26), custom_call_target="tpu_custom_call" | custom-call | flops 20000000000 | bytes 66666664 | tf_op jit(solution)/shard_map/final/pallas_call | solution.py:207
  (1 shorter events, 0.0 us)
Async XLA Ops:
  0.0 0.7 %copy-start.3 = (s32[1,1,32,4]{2,3,1,0:T(4,128)S(1)}, s32[1,1,32,4]{2,3,1,0:T(4,128)}, u32[]{:S(2)}) copy-start(s32[1,1,32,4]{2,3,1,0:T(4,128)} %param.12) | copy-start | bytes 1540
  0.0 0.7 %copy-start.5 = (s32[1,1,32]{2,1,0:T(1,128)S(1)}, s32[1,1,32]{2,1,0:T(1,128)}, u32[]{:S(2)}) copy-start(s32[1,1,32]{2,1,0:T(1,128)} %param.11) | copy-start | bytes 388
  0.0 0.7 %copy-start.4 = (s32[1,1,32]{2,1,0:T(1,128)S(1)}, s32[1,1,32]{2,1,0:T(1,128)}, u32[]{:S(2)}) copy-start(s32[1,1,32]{2,1,0:T(1,128)} %param.10) | copy-start | bytes 388
  0.0 0.8 %copy-start.2 = (f32[32,1,128]{2,1,0:T(1,128)S(1)}, f32[32,1,128]{2,1,0:T(1,128)}, u32[]{:S(2)}) copy-start(f32[32,1,128]{2,1,0:T(1,128)} %param.8) | copy-start | bytes 49156
  0.8 12.6 %copy-start = (f32[1,1,32,4,128,128]{5,4,3,2,1,0:T(8,128)S(1)}, f32[1,1,32,4,128,128]{5,4,3,2,1,0:T(8,128)}, u32[]{:S(2)}) copy-start(f32[1,1,32,4,128,128]{5,4,3,2,1,0:T(8,128)} %param.13) | copy-start | bytes 25165828
  28.2 11.8 %copy-start.1 = (f32[1,128,128]{2,1,0:T(8,128)S(1)}, f32[1,128,128]{2,1,0:T(8,128)}, u32[]{:S(2)}) copy-start(f32[1,128,128]{2,1,0:T(8,128)} %param.15) | copy-start | bytes 196612
  28.2 11.8 %copy-start.6 = (f32[1,128]{1,0:T(1,128)S(1)}, f32[1,128]{1,0:T(1,128)}, u32[]{:S(2)}) copy-start(f32[1,128]{1,0:T(1,128)} %incident_ref.1) | copy-start | bytes 1540
